TPU v7x, 128 devices: a whole 4x4x4 slice. The times are simulated.
128 devices in a mesh: dp: 16 (over x, y_hi, core), fsdp: 8 (over y_lo, z).
Axes of the slice: x: 4, y: 4 (y_hi: 2, y_lo: 2; y = y_hi * 2 + y_lo), z: 4, core: 2. Of those that a mesh axis runs over, the one named last changes fastest.
Arguments:
- tokens: bfloat16 [32768, 768], P(('dp', 'fsdp')), may hold values from -6 to 6
- lengths: int32 [128], P(('dp', 'fsdp')), may hold values from 128 to 256, as said below
- cotangent: bfloat16 [32768, 768], P(('dp', 'fsdp')), may hold values from -24 to 24
- joint_weight: float32 [2, 768, 2304], P(None, None, ('dp', 'fsdp')), may hold values from -0.21875 to 0.21875
- output_weight: float32 [2, 768, 768], P(None, None, ('dp', 'fsdp')), may hold values from -0.4375 to 0.4375
- expand_weight: float32 [2, 768, 3072], P(None, None, ('dp', 'fsdp')), may hold values from -0.21875 to 0.21875
- shrink_weight: float32 [2, 3072, 768], P(None, ('dp', 'fsdp')), may hold values from -0.109375 to 0.109375
- layer_gains: float32 [2, 4, 768], P(None, None, ('dp', 'fsdp')), may hold values from -0.3 to 1.4
- joint_moment: float32 [2, 768, 2304], P(None, None, ('dp', 'fsdp')), may hold values from -0.00021922641 to 0.00021922641
- output_moment: float32 [2, 768, 768], P(None, None, ('dp', 'fsdp')), may hold values from -7.0152453e-05 to 7.0152453e-05
- expand_moment: float32 [2, 768, 3072], P(None, None, ('dp', 'fsdp')), may hold values from -6.13834e-05 to 6.13834e-05
- shrink_moment: float32 [2, 3072, 768], P(None, ('dp', 'fsdp')), may hold values from -8.769057e-05 to 8.769057e-05
- gains_moment: float32 [2, 4, 768], P(None, None, ('dp', 'fsdp')), may hold values from -0.0002630717 to 0.0002630717
- joint_square: float32 [2, 768, 2304], P(None, None, ('dp', 'fsdp')), may hold values from 1.76529736e-11 to 1.7652974e-09
- output_square: float32 [2, 768, 768], P(None, None, ('dp', 'fsdp')), may hold values from 4.519161e-11 to 1.8076645e-10
- expand_square: float32 [2, 768, 3072], P(None, None, ('dp', 'fsdp')), may hold values from 3.459983e-11 to 1.38399313e-10
- shrink_square: float32 [2, 3072, 768], P(None, ('dp', 'fsdp')), may hold values from 7.061189e-11 to 2.82447578e-10
- gains_square: float32 [2, 4, 768], P(None, None, ('dp', 'fsdp')), may hold values from 6.3550705e-10 to 2.5420282e-09
Outputs:
- layer_output: bfloat16 [32768, 768], P(('dp', 'fsdp'))
- input_gradient: float32 [32768, 768], P(('dp', 'fsdp'))
- gradient_norm: float32 [], replicated
- joint_master: float32 [2, 768, 2304], P(None, None, ('dp', 'fsdp'))
- output_master: float32 [2, 768, 768], P(None, None, ('dp', 'fsdp'))
- expand_master: float32 [2, 768, 3072], P(None, None, ('dp', 'fsdp'))
- shrink_master: float32 [2, 3072, 768], P(None, ('dp', 'fsdp'))
- gains_master: float32 [2, 4, 768], P(None, None, ('dp', 'fsdp'))
- joint_momentum: float32 [2, 768, 2304], P(None, None, ('dp', 'fsdp'))
- output_momentum: float32 [2, 768, 768], P(None, None, ('dp', 'fsdp'))
- expand_momentum: float32 [2, 768, 3072], P(None, None, ('dp', 'fsdp'))
- shrink_momentum: float32 [2, 3072, 768], P(None, ('dp', 'fsdp'))
- gains_momentum: float32 [2, 4, 768], P(None, None, ('dp', 'fsdp'))
- joint_variance: float32 [2, 768, 2304], P(None, None, ('dp', 'fsdp'))
- output_variance: float32 [2, 768, 768], P(None, None, ('dp', 'fsdp'))
- expand_variance: float32 [2, 768, 3072], P(None, None, ('dp', 'fsdp'))
- shrink_variance: float32 [2, 3072, 768], P(None, ('dp', 'fsdp'))
- gains_variance: float32 [2, 4, 768], P(None, None, ('dp', 'fsdp'))
Inputs may be any that keep to these rules, and one draw needn't show every extreme that they name: The sequence of device d fills its first lengths[d] slots; the later slots are padding.
All inputs are finite; a program needn't handle non-finite values.
Results may differ from a plain program's by a relative error of at most 0.017.
Values may be sent and summed in bfloat16 or wider, within the bound.
A program may use at most 256 MiB of HBM per device.

v0:
```python
import jax
import jax.numpy as jnp
from jax import lax
from jax.sharding import PartitionSpec as P

D = 768
HEADS = 12
HEAD_DIM = 64
LAYERS = 2
STEP = 5


highest = lax.Precision.HIGHEST
beta_first = 0.9
beta_second = 0.999
adam_epsilon = 1e-08
decay_matrix = 0.1
rate_matrix = 0.05
rate_gains = 0.25
clip_limit = 1.0
norm_epsilon = 1e-05
masked_value = -1e30


def layer_norm(features, gain_row, shift_row):
    mean_value = jnp.mean(features, axis=-1, keepdims=True)
    centred = features - mean_value
    variance = jnp.mean(centred * centred, axis=-1, keepdims=True)
    return centred * lax.rsqrt(variance + norm_epsilon) * gain_row + shift_row


def gelu_tanh(raised):
    return jax.nn.gelu(raised, approximate=True)


def adam_update(master, gradient, moment, square, rate, decay, clip_factor):
    clipped = gradient * clip_factor
    momentum = beta_first * moment + (1.0 - beta_first) * clipped
    variance = beta_second * square + (1.0 - beta_second) * clipped * clipped
    corrected_first = momentum / (1.0 - beta_first**STEP)
    corrected_second = variance / (1.0 - beta_second**STEP)
    updated = master - rate * (
        corrected_first / (jnp.sqrt(corrected_second) + adam_epsilon) + decay * master
    )
    return (updated, momentum, variance)


def split_heads(projected, offset):
    row_count = projected.shape[0]
    return projected[:, offset * D : (offset + 1) * D].reshape(row_count, HEADS, HEAD_DIM)


def attention_logits(query_rows, key_rows, masks):
    allowed, selectable, earlier = masks
    scores = jnp.einsum(
        "ihd,jhd->hij", query_rows, key_rows, preferred_element_type=jnp.float32
    ) * HEAD_DIM ** (-0.5)
    chosen = jnp.where(selectable, jax.nn.softplus(scores[0]), 0.0)
    forget = jnp.dot(earlier, chosen, precision=highest)
    logits = jnp.where(allowed[None], scores - forget[None], masked_value)
    return (scores, logits)


def fetch(masters, which_layer):
    joint_piece = masters[0][which_layer].astype(jnp.bfloat16)
    output_piece = masters[1][which_layer].astype(jnp.bfloat16)
    expand_piece = masters[2][which_layer].astype(jnp.bfloat16)
    shrink_piece = masters[3][which_layer].astype(jnp.bfloat16)
    gains_piece = masters[4][which_layer].astype(jnp.bfloat16)
    return (
        lax.all_gather(joint_piece, ("dp", "fsdp"), axis=1, tiled=True),
        lax.all_gather(output_piece, ("dp", "fsdp"), axis=1, tiled=True),
        lax.all_gather(expand_piece, ("dp", "fsdp"), axis=1, tiled=True),
        lax.all_gather(shrink_piece, ("dp", "fsdp"), axis=0, tiled=True),
        lax.all_gather(gains_piece, ("dp", "fsdp"), axis=1, tiled=True),
    )


def reduce_grads(gradients):
    joint_grad, output_grad, expand_grad, shrink_grad, gains_grad = gradients
    return (
        lax.psum_scatter(joint_grad, ("dp", "fsdp"), scatter_dimension=1, tiled=True),
        lax.psum_scatter(output_grad, ("dp", "fsdp"), scatter_dimension=1, tiled=True),
        lax.psum_scatter(expand_grad, ("dp", "fsdp"), scatter_dimension=1, tiled=True),
        lax.psum_scatter(shrink_grad, ("dp", "fsdp"), scatter_dimension=0, tiled=True),
        lax.psum_scatter(gains_grad, ("dp", "fsdp"), scatter_dimension=1, tiled=True),
    )


def layer_forward(stream, weights, masks):
    joint_full, output_full, expand_full, shrink_full, gains_full = weights
    row_count = stream.shape[0]
    gains = gains_full.astype(jnp.float32)
    normed = layer_norm(stream, gains[0], gains[1]).astype(jnp.bfloat16)
    projected = jnp.dot(normed, joint_full, preferred_element_type=jnp.float32).astype(jnp.bfloat16)
    query_rows = split_heads(projected, 0)
    key_rows = split_heads(projected, 1)
    value_rows = split_heads(projected, 2)
    scores, logits = attention_logits(query_rows, key_rows, masks)
    row_max = jnp.max(logits, axis=-1, keepdims=True)
    shifted = jnp.exp(logits - row_max)
    row_total = jnp.sum(shifted, axis=-1, keepdims=True)
    softmax_low = (shifted / row_total).astype(jnp.bfloat16)
    log_total = row_max + jnp.log(row_total)
    attended = jnp.einsum(
        "hij,jhd->ihd", softmax_low, value_rows, preferred_element_type=jnp.float32
    )
    attended = attended.reshape(row_count, D).astype(jnp.bfloat16)
    stream_mid = stream + jnp.dot(attended, output_full, preferred_element_type=jnp.float32)
    normed_second = layer_norm(stream_mid, gains[2], gains[3]).astype(jnp.bfloat16)
    raised = jnp.dot(normed_second, expand_full, preferred_element_type=jnp.float32)
    hidden = gelu_tanh(raised).astype(jnp.bfloat16)
    stream_next = stream_mid + jnp.dot(hidden, shrink_full, preferred_element_type=jnp.float32)
    saved = (
        stream,
        normed,
        projected,
        log_total,
        attended,
        stream_mid,
        normed_second,
        raised,
        hidden,
    )
    return (stream_next, saved)


def layer_backward(dstream, weights, saved, masks):
    joint_full, output_full, expand_full, shrink_full, gains_full = weights
    stream, normed, projected, log_total, attended, stream_mid, normed_second, raised, hidden = (
        saved
    )
    allowed, selectable, earlier = masks
    row_count = stream.shape[0]
    gains = gains_full.astype(jnp.float32)
    dbranch = dstream.astype(jnp.bfloat16)
    shrink_grad = jnp.einsum("tf,td->fd", hidden, dbranch, preferred_element_type=jnp.float32)
    dhidden = jnp.einsum("td,fd->tf", dbranch, shrink_full, preferred_element_type=jnp.float32)
    gelu_value, gelu_pull = jax.vjp(gelu_tanh, raised)
    draised = gelu_pull(dhidden)[0].astype(jnp.bfloat16)
    expand_grad = jnp.einsum(
        "te,tf->ef", normed_second, draised, preferred_element_type=jnp.float32
    )
    dnormed_second = jnp.einsum(
        "tf,ef->te", draised, expand_full, preferred_element_type=jnp.float32
    )
    second_value, second_pull = jax.vjp(layer_norm, stream_mid, gains[2], gains[3])
    dmiddle, dgain_second, dshift_second = second_pull(dnormed_second)
    dstream_mid = dstream + dmiddle
    dattn = dstream_mid.astype(jnp.bfloat16)
    output_grad = jnp.einsum("te,td->ed", attended, dattn, preferred_element_type=jnp.float32)
    dattended = jnp.einsum("td,ed->te", dattn, output_full, preferred_element_type=jnp.float32)
    dattended = dattended.astype(jnp.bfloat16).reshape(row_count, HEADS, HEAD_DIM)
    query_rows = split_heads(projected, 0)
    key_rows = split_heads(projected, 1)
    value_rows = split_heads(projected, 2)
    scores, logits = attention_logits(query_rows, key_rows, masks)
    softmax_full = jnp.exp(logits - log_total)
    softmax_low = softmax_full.astype(jnp.bfloat16)
    dsoft = jnp.einsum("ihd,jhd->hij", dattended, value_rows, preferred_element_type=jnp.float32)
    dvalues = jnp.einsum("hij,ihd->jhd", softmax_low, dattended, preferred_element_type=jnp.float32)
    dlogits = softmax_full * (dsoft - jnp.sum(softmax_full * dsoft, axis=-1, keepdims=True))
    dforget = -jnp.sum(dlogits, axis=0)
    dchosen = jnp.dot(earlier.T, dforget, precision=highest)
    slope = jax.nn.sigmoid(scores[0])
    head_zero = dlogits[0] + jnp.where(selectable, dchosen * slope, 0.0)
    dscores = jnp.concatenate([head_zero[None], dlogits[1:]], axis=0).astype(jnp.bfloat16)
    score_scale = HEAD_DIM ** (-0.5)
    dqueries = (
        jnp.einsum("hij,jhd->ihd", dscores, key_rows, preferred_element_type=jnp.float32)
        * score_scale
    )
    dkeys = (
        jnp.einsum("hij,ihd->jhd", dscores, query_rows, preferred_element_type=jnp.float32)
        * score_scale
    )
    dprojected = jnp.concatenate(
        [
            dqueries.reshape(row_count, D),
            dkeys.reshape(row_count, D),
            dvalues.reshape(row_count, D),
        ],
        axis=1,
    ).astype(jnp.bfloat16)
    joint_grad = jnp.einsum("te,tc->ec", normed, dprojected, preferred_element_type=jnp.float32)
    dnormed = jnp.einsum("tc,ec->te", dprojected, joint_full, preferred_element_type=jnp.float32)
    first_value, first_pull = jax.vjp(layer_norm, stream, gains[0], gains[1])
    dinput, dgain_first, dshift_first = first_pull(dnormed)
    dstream_in = dstream_mid + dinput
    gains_grad = jnp.stack([dgain_first, dshift_first, dgain_second, dshift_second])
    return (dstream_in, (joint_grad, output_grad, expand_grad, shrink_grad, gains_grad))


def local(
    tokens,
    lengths,
    cotangent,
    joint_weight,
    output_weight,
    expand_weight,
    shrink_weight,
    layer_gains,
    joint_moment,
    output_moment,
    expand_moment,
    shrink_moment,
    gains_moment,
    joint_square,
    output_square,
    expand_square,
    shrink_square,
    gains_square,
):
    row_count = tokens.shape[0]
    positions = jnp.arange(row_count, dtype=jnp.int32)
    live_rows = positions < lengths[0]
    allowed = (positions[None, :] <= positions[:, None]) & live_rows[None, :]
    selectable = (
        (positions[None, :] > 0) & (positions[None, :] < positions[:, None]) & live_rows[:, None]
    )
    earlier = (positions[None, :] < positions[:, None]).astype(jnp.float32)
    masks = (allowed, selectable, earlier)
    masters = (joint_weight, output_weight, expand_weight, shrink_weight, layer_gains)
    stream = tokens.astype(jnp.float32)
    saved_layers = []
    for which_layer in range(LAYERS):
        weights = fetch(masters, which_layer)
        stream, saved = layer_forward(stream, weights, masks)
        saved_layers.append(saved)
    layer_output = stream.astype(jnp.bfloat16)
    dstream = cotangent.astype(jnp.float32) * live_rows[:, None].astype(jnp.float32)
    reduced = [None] * LAYERS
    for which_layer in reversed(range(LAYERS)):
        weights = fetch(masters, which_layer)
        dstream, gradients = layer_backward(dstream, weights, saved_layers[which_layer], masks)
        reduced[which_layer] = reduce_grads(gradients)
    stacked = [
        jnp.stack([reduced[which_layer][which_kind] for which_layer in range(LAYERS)])
        for which_kind in range(5)
    ]
    local_square = (
        jnp.sum(stacked[0] * stacked[0])
        + jnp.sum(stacked[1] * stacked[1])
        + jnp.sum(stacked[2] * stacked[2])
        + jnp.sum(stacked[3] * stacked[3])
        + jnp.sum(stacked[4] * stacked[4])
    )
    total_square = lax.psum(local_square, ("dp", "fsdp"))
    gradient_norm = jnp.sqrt(total_square)
    clip_factor = jnp.minimum(1.0, clip_limit / (gradient_norm + 1e-06))
    joint_new = adam_update(
        joint_weight, stacked[0], joint_moment, joint_square, rate_matrix, decay_matrix, clip_factor
    )
    output_new = adam_update(
        output_weight,
        stacked[1],
        output_moment,
        output_square,
        rate_matrix,
        decay_matrix,
        clip_factor,
    )
    expand_new = adam_update(
        expand_weight,
        stacked[2],
        expand_moment,
        expand_square,
        rate_matrix,
        decay_matrix,
        clip_factor,
    )
    shrink_new = adam_update(
        shrink_weight,
        stacked[3],
        shrink_moment,
        shrink_square,
        rate_matrix,
        decay_matrix,
        clip_factor,
    )
    gains_new = adam_update(
        layer_gains, stacked[4], gains_moment, gains_square, rate_gains, 0.0, clip_factor
    )
    return (
        layer_output,
        dstream,
        gradient_norm,
        joint_new[0],
        output_new[0],
        expand_new[0],
        shrink_new[0],
        gains_new[0],
        joint_new[1],
        output_new[1],
        expand_new[1],
        shrink_new[1],
        gains_new[1],
        joint_new[2],
        output_new[2],
        expand_new[2],
        shrink_new[2],
        gains_new[2],
    )


def solution(mesh):
    in_specs = (
        P(("dp", "fsdp"), None),
        P(("dp", "fsdp")),
        P(("dp", "fsdp"), None),
        P(None, None, ("dp", "fsdp")),
        P(None, None, ("dp", "fsdp")),
        P(None, None, ("dp", "fsdp")),
        P(None, ("dp", "fsdp"), None),
        P(None, None, ("dp", "fsdp")),
        P(None, None, ("dp", "fsdp")),
        P(None, None, ("dp", "fsdp")),
        P(None, None, ("dp", "fsdp")),
        P(None, ("dp", "fsdp"), None),
        P(None, None, ("dp", "fsdp")),
        P(None, None, ("dp", "fsdp")),
        P(None, None, ("dp", "fsdp")),
        P(None, None, ("dp", "fsdp")),
        P(None, ("dp", "fsdp"), None),
        P(None, None, ("dp", "fsdp")),
    )
    out_specs = (
        P(("dp", "fsdp"), None),
        P(("dp", "fsdp"), None),
        P(),
        P(None, None, ("dp", "fsdp")),
        P(None, None, ("dp", "fsdp")),
        P(None, None, ("dp", "fsdp")),
        P(None, ("dp", "fsdp"), None),
        P(None, None, ("dp", "fsdp")),
        P(None, None, ("dp", "fsdp")),
        P(None, None, ("dp", "fsdp")),
        P(None, None, ("dp", "fsdp")),
        P(None, ("dp", "fsdp"), None),
        P(None, None, ("dp", "fsdp")),
        P(None, None, ("dp", "fsdp")),
        P(None, None, ("dp", "fsdp")),
        P(None, None, ("dp", "fsdp")),
        P(None, ("dp", "fsdp"), None),
        P(None, None, ("dp", "fsdp")),
    )
    return jax.shard_map(local, mesh=mesh, in_specs=in_specs, out_specs=out_specs, check_vma=False)
```

profile of v0, /device:TPU:1, one launch (start us, length us, event | category | flops | bytes accessed | tf_op | source)
XLA Modules:
  0.0 5236.7 jit_solution(3336423681336168582)
XLA Ops:
  21.8 304.7 %all-gather.5 = bf16[1,4,768]{1,0,2:T(2,128)(2,1)S(1)} all-gather(bf16[1,4,6]{1,0,2:T(2,128)(2,1)S(1)} %get-tuple-element.159), channel_id=7, replica_groups=mesh['dp'=16,'fsdp'=8] {'dp','fsdp'}, dimensions={2}, use_global_device_ids=true | all-gather | bytes 6192 | tf_op jit(solution)/shard_map/all_gather | solution.py:75
  326.9 10.4 slice_reduce_fusion.1
  337.2 312.4 %all-gather = bf16[1,4,768]{1,0,2:T(2,128)(2,1)S(1)} all-gather(bf16[1,4,6]{1,0,2:T(2,128)(2,1)S(1)} %get-tuple-element.160), channel_id=2, replica_groups=mesh['dp'=16,'fsdp'=8] {'dp','fsdp'}, dimensions={2}, use_global_device_ids=true | all-gather | bytes 6192 | tf_op jit(solution)/shard_map/all_gather | solution.py:75
  650.6 10.3 slice_reduce_fusion.5
  661.0 6.4 copy.167
  667.5 6.4 copy.160
  673.9 257.0 %all-gather.19.cloned.1.call-done = bf16[1,768,2304]{1,0,2:T(2,128)(2,1)} async-done(((bf16[1,768,18]{1,0,2:T(2,128)(2,1)}), bf16[1,768,2304]{1,0,2:T(2,128)(2,1)}) %all-gather.19.cloned.1.call-update) | async-done | bytes 3538960 | tf_op jit(solution)/shard_map/all_gather | solution.py:71
  930.9 15.9 copy.154
  952.9 289.7 %all-gather.27.cloned.1.call-done = bf16[1,768,2304]{1,0,2:T(2,128)(2,1)} async-done(((bf16[1,768,18]{1,0,2:T(2,128)(2,1)}), bf16[1,768,2304]{1,0,2:T(2,128)(2,1)}) %all-gather.27.cloned.1.call-update) | async-done | bytes 3538960 | tf_op jit(solution)/shard_map/all_gather | solution.py:71
  1242.5 16.1 copy.161
  1266.1 286.2 %all-gather.23.cloned.1.call-done = bf16[1,768,3072]{1,2,0:T(8,128)(2,1)} async-done(((bf16[1,768,24]{1,2,0:T(8,128)(2,1)}), bf16[1,768,3072]{1,2,0:T(8,128)(2,1)}) %all-gather.23.cloned.1.call-update) | async-done | bytes 4718608 | tf_op jit(solution)/shard_map/all_gather | solution.py:73
  1552.4 5.8 fusion.18
  1558.2 305.8 %all-gather.25.cloned.1.call-done = bf16[1,3072,768]{2,1,0:T(8,128)(2,1)} async-done(((bf16[1,24,768]{2,1,0:T(8,128)(2,1)}), bf16[1,3072,768]{2,1,0:T(8,128)(2,1)}) %all-gather.25.cloned.1.call-update) | async-done | bytes 4718608 | tf_op jit(solution)/shard_map/all_gather | solution.py:74
  1864.0 5.6 fusion.198
  1885.9 290.2 %all-gather.31.cloned.1.call-done = bf16[1,768,3072]{1,2,0:T(8,128)(2,1)} async-done(((bf16[1,768,24]{1,2,0:T(8,128)(2,1)}), bf16[1,768,3072]{1,2,0:T(8,128)(2,1)}) %all-gather.31.cloned.1.call-update) | async-done | bytes 4718608 | tf_op jit(solution)/shard_map/all_gather | solution.py:73
  2176.1 5.9 fusion.10
  2182.0 305.3 %all-gather.33.cloned.1.call-done = bf16[1,3072,768]{2,1,0:T(8,128)(2,1)} async-done(((bf16[1,24,768]{2,1,0:T(8,128)(2,1)}), bf16[1,3072,768]{2,1,0:T(8,128)(2,1)}) %all-gather.33.cloned.1.call-update) | async-done | bytes 4718608 | tf_op jit(solution)/shard_map/all_gather | solution.py:74
  2487.3 6.2 fusion.39
  2514.1 6.3 fusion.132
  2520.5 7.9 fusion.135
  2528.4 6.3 fusion.32
  2536.0 5.1 fusion.175
  2541.8 6.8 fusion.176
  2550.0 5.3 multiply_reduce_fusion.4
  2570.4 4.1 fusion.101
  2574.5 4.0 fusion.102
  2578.6 379.6 %fusion.177 = (f32[768,24]{0,1:T(8,128)}, f32[768,24]{0,1:T(8,128)}, f32[768,8]{0,1:T(8,128)}, f32[768,8]{0,1:T(8,128)}) fusion(f32[768,2304]{0,1:T(8,128)} %fusion.102, f32[768,2304]{0,1:T(8,128)} %fusion.101, f32[768,768]{0,1:T(8,128)S(1)} %copy-done.21, f32[768,768]{0,1:T(8,128)} %fusion.129), kind=kCustom, calls=%all-reduce-scatter.4 | all-reduce-scatter fusion | flops 6291458 | bytes 19070976
  2966.2 22.3 collective-permute-start.123
  2998.9 6.7 collective-permute-start.116
  3008.0 4.0 collective-permute-start.114
  3017.5 4.6 collective-permute-start.110
  3022.2 4.3 collective-permute-start.109
  3040.5 4.0 collective-permute-start.102
  3051.3 5.0 collective-permute-start.98
  3076.5 4.4 collective-permute-start.86
  3095.0 3.7 collective-permute-start.78
  3124.5 5.0 collective-permute-start.66
  3138.8 6.1 collective-permute-done.65
  3146.8 6.0 collective-permute-done.64
  3161.2 5.3 collective-permute-start.55
  3171.9 6.0 fusion.62
  3178.1 3.7 collective-permute-start.50
  3187.0 3.4 collective-permute-start.47
  3191.2 3.8 collective-permute-start.46
  3211.7 3.7 collective-permute-start.38
  3222.6 4.3 collective-permute-start.34
  3237.8 3.4 collective-permute-start.26
  3248.5 4.5 collective-permute-start.22
  3257.0 64.2 %all-reduce.10 = (f32[4,768]{1,0:T(4,128)S(1)}, f32[4,768]{1,0:T(4,128)S(1)}) all-reduce(f32[4,768]{1,0:T(4,128)S(1)} %pad_maximum_fusion.17, f32[4,768]{1,0:T(4,128)S(1)} %pad_maximum_fusion.16), channel_id=21, replica_groups=mesh['dp'=16,'fsdp'=8] {'dp','fsdp'}, use_global_device_ids=true, to_apply=%region_45.46.clone | all-reduce | flops 6144 | bytes 49152
  3324.4 4.4 collective-permute-start.18
  3328.9 3.8 collective-permute-start.17
  3335.1 4.5 collective-permute-start.15
  3339.7 6.6 collective-permute-start.14
  3346.3 4.4 collective-permute-start.13
  3359.4 47.1 concatenate.23
  3406.5 26.5 concatenate.22
  3439.2 4.0 collective-permute-start.6
  3450.8 5.1 collective-permute-start.2
  3461.2 47.8 concatenate.21
  3509.0 48.3 concatenate.20
  3561.3 273.1 %reduce-scatter.21.cloned.1.call-done = f32[24,768]{1,0:T(8,128)} async-done(((f32[3072,768]{1,0:T(8,128)}), f32[24,768]{1,0:T(8,128)}) %reduce-scatter.21.cloned.1.call-update) | async-done | bytes 73744 | tf_op jit(solution)/shard_map/reduce_scatter | solution.py:85
  3836.1 649.2 %reduce-scatter.15.cloned.1.call-done = f32[768,24]{0,1:T(8,128)} async-done(((f32[768,3072]{0,1:T(8,128)}), f32[768,24]{0,1:T(8,128)}) %reduce-scatter.15.cloned.1.call-update) | async-done | bytes 73744 | tf_op jit(solution)/shard_map/reduce_scatter | solution.py:84
  4485.3 650.8 %reduce-scatter.17.cloned.1.call-done = f32[768,24]{0,1:T(8,128)} async-done(((f32[768,3072]{0,1:T(8,128)}), f32[768,24]{0,1:T(8,128)}) %reduce-scatter.17.cloned.1.call-update) | async-done | bytes 73744 | tf_op jit(solution)/shard_map/reduce_scatter | solution.py:84
  5140.8 78.3 %psum.7 = f32[]{:T(128)} all-reduce(f32[]{:T(128)S(6)} %add.314), channel_id=1, replica_groups=mesh['dp'=16,'fsdp'=8] {'dp','fsdp'}, use_global_device_ids=true, to_apply=%region_47.48 | all-reduce | flops 1 | bytes 8 | tf_op jit(solution)/shard_map/psum | solution.py:248
  (887 shorter events, 313.3 us)
Async XLA Ops:
  7.2 653.8 %all-gather.29.cloned.1.call-start = ((), (), s32[]{:S(2)}) async-start(), calls=%async_computation.13 | async-start | bytes 2377728 | tf_op jit(solution)/shard_map/all_gather | solution.py:72
  8.7 658.8 %all-gather.21.cloned.1.call-start = ((), (), s32[]{:S(2)}) async-start(), calls=%async_computation.9 | async-start | bytes 2377728 | tf_op jit(solution)/shard_map/all_gather | solution.py:72
  9.4 921.4 %all-gather.19.cloned.1.call-start = ((), (), s32[]{:S(2)}) async-start(), calls=%async_computation.8 | async-start | bytes 7133184 | tf_op jit(solution)/shard_map/all_gather | solution.py:71
  11.2 1231.4 %all-gather.27.cloned.1.call-start = ((), (), s32[]{:S(2)}) async-start(), calls=%async_computation.12 | async-start | bytes 7133184 | tf_op jit(solution)/shard_map/all_gather | solution.py:71
  11.8 1540.6 %all-gather.23.cloned.1.call-start = ((), (), s32[]{:S(2)}) async-start(), calls=%async_computation.10 | async-start | bytes 4755456 | tf_op jit(solution)/shard_map/all_gather | solution.py:73
  13.4 1850.6 %all-gather.25.cloned.1.call-start = ((), (), s32[]{:S(2)}) async-start(), calls=%async_computation.11 | async-start | bytes 4755456 | tf_op jit(solution)/shard_map/all_gather | solution.py:74
  15.0 2161.1 %all-gather.31.cloned.1.call-start = ((), (), s32[]{:S(2)}) async-start(), calls=%async_computation.14 | async-start | bytes 4755456 | tf_op jit(solution)/shard_map/all_gather | solution.py:73
  15.8 2471.5 %all-gather.33.cloned.1.call-start = ((), (), s32[]{:S(2)}) async-start(), calls=%async_computation.15 | async-start | bytes 4755456 | tf_op jit(solution)/shard_map/all_gather | solution.py:74
  16.5 3544.8 %reduce-scatter.19.cloned.1.call-start = ((), (), s32[]{:S(2)}) async-start(), calls=%async_computation.6 | async-start | bytes 9510912 | tf_op jit(solution)/shard_map/reduce_scatter | solution.py:85
  2520.4 1314.0 %reduce-scatter.21.cloned.1.call-start = ((), (), s32[]{:S(2)}) async-start(), calls=%async_computation.7 | async-start | bytes 9510912 | tf_op jit(solution)/shard_map/reduce_scatter | solution.py:85
  2528.4 1956.9 %reduce-scatter.15.cloned.1.call-start = ((), (), s32[]{:S(2)}) async-start(), calls=%async_computation.4 | async-start | bytes 9510912 | tf_op jit(solution)/shard_map/reduce_scatter | solution.py:84
  2541.1 2594.9 %reduce-scatter.17.cloned.1.call-start = ((), (), s32[]{:S(2)}) async-start(), calls=%async_computation.5 | async-start | bytes 9510912 | tf_op jit(solution)/shard_map/reduce_scatter | solution.py:84
  2960.2 31.1 collective-permute-start.126
  2961.5 32.1 collective-permute-start.125
  2963.6 24.9 collective-permute-start.127
  2964.9 30.1 collective-permute-start.124
  2966.2 30.1 collective-permute-start.123
  2996.3 15.7 collective-permute-start.118
  2997.6 16.4 collective-permute-start.117
  2998.9 16.4 collective-permute-start.116
  3012.0 14.5 collective-permute-start.113
  3014.0 14.5 collective-permute-start.112
  3015.3 15.8 collective-permute-start.111
  3017.5 16.4 collective-permute-start.110
  3040.5 15.8 collective-permute-start.102
  3115.0 14.5 collective-permute-start.70
  3129.5 28.6 collective-permute-start.62
  3130.9 28.5 collective-permute-start.61
  3134.0 20.1 collective-permute-start.31
  3135.4 20.7 collective-permute-start.63
  3161.2 16.9 collective-permute-start.55
  3166.5 15.3 collective-permute-start.54
  3167.9 16.3 collective-permute-start.53
  3169.2 17.8 collective-permute-start.52
  3170.6 19.9 collective-permute-start.51
  3178.1 18.3 collective-permute-start.50
  3181.9 16.8 collective-permute-start.49
  3184.2 16.4 collective-permute-start.48
  3187.0 15.2 collective-permute-start.47
  3191.2 14.5 collective-permute-start.46
  3211.7 15.2 collective-permute-start.38
  3237.8 15.2 collective-permute-start.26
  3244.2 76.9 %collective-permute-start.24 = (f32[768,24]{0,1:T(8,128)S(1)}, f32[768,24]{0,1:T(8,128)}, u32[]{:S(2)}, u32[]{:S(2)}) collective-permute-start(f32[768,24]{0,1:T(8,128)S(1)} %copy-done.57), channel_id=1, source_target_pairs={{0,25},{1,26},{2,27},{3,28},{4,29},{5,30},{6,31},{7,32},{8,33},{9,... | collective-permute-start | bytes 221192
  3246.2 78.3 %collective-permute-start.23 = (f32[768,24]{0,1:T(8,128)S(1)}, f32[768,24]{0,1:T(8,128)}, u32[]{:S(2)}, u32[]{:S(2)}) collective-permute-start(f32[768,24]{0,1:T(8,128)S(1)} %copy-done.57), channel_id=1, source_target_pairs={{0,24},{1,25},{2,26},{3,27},{4,28},{5,29},{6,30},{7,31},{8,32},{9,... | collective-permute-start | bytes 221192
  3248.5 80.4 %collective-permute-start.22 = (f32[768,24]{0,1:T(8,128)S(1)}, f32[768,24]{0,1:T(8,128)}, u32[]{:S(2)}, u32[]{:S(2)}) collective-permute-start(f32[768,24]{0,1:T(8,128)S(1)} %copy-done.57), channel_id=1, source_target_pairs={{0,23},{1,24},{2,25},{3,26},{4,27},{5,28},{6,29},{7,30},{8,31},{9,... | collective-permute-start | bytes 221192
  3253.0 79.7 %collective-permute-start.21 = (f32[768,24]{0,1:T(8,128)S(1)}, f32[768,24]{0,1:T(8,128)}, u32[]{:S(2)}, u32[]{:S(2)}) collective-permute-start(f32[768,24]{0,1:T(8,128)S(1)} %copy-done.57), channel_id=1, source_target_pairs={{0,22},{1,23},{2,24},{3,25},{4,26},{5,27},{6,28},{7,29},{8,30},{9,... | collective-permute-start | bytes 221192
  3254.9 80.2 %collective-permute-start.20 = (f32[768,24]{0,1:T(8,128)S(1)}, f32[768,24]{0,1:T(8,128)}, u32[]{:S(2)}, u32[]{:S(2)}) collective-permute-start(f32[768,24]{0,1:T(8,128)S(1)} %copy-done.57), channel_id=1, source_target_pairs={{0,21},{1,22},{2,23},{3,24},{4,25},{5,26},{6,27},{7,28},{8,29},{9,... | collective-permute-start | bytes 221192
  3321.1 18.6 collective-permute-start.19
  3324.4 21.9 collective-permute-start.18
  3328.9 21.8 collective-permute-start.17
  3332.7 21.0 collective-permute-start.16
  3335.1 20.5 collective-permute-start.15
  3339.7 93.2 %collective-permute-start.14 = (f32[768,24]{0,1:T(8,128)S(1)}, f32[768,24]{0,1:T(8,128)}, u32[]{:S(2)}, u32[]{:S(2)}) collective-permute-start(f32[768,24]{0,1:T(8,128)S(1)} %copy-done.57), channel_id=1, source_target_pairs={{0,15},{1,16},{2,17},{3,18},{4,19},{5,20},{6,21},{7,22},{8,23},{9,... | collective-permute-start | bytes 221192
  3346.3 88.9 %collective-permute-start.13 = (f32[768,24]{0,1:T(8,128)S(1)}, f32[768,24]{0,1:T(8,128)}, u32[]{:S(2)}, u32[]{:S(2)}) collective-permute-start(f32[768,24]{0,1:T(8,128)S(1)} %copy-done.57), channel_id=1, source_target_pairs={{0,14},{1,15},{2,16},{3,17},{4,18},{5,19},{6,20},{7,21},{8,22},{9,... | collective-permute-start | bytes 221192
  3350.7 86.5 %collective-permute-start.12 = (f32[768,24]{0,1:T(8,128)S(1)}, f32[768,24]{0,1:T(8,128)}, u32[]{:S(2)}, u32[]{:S(2)}) collective-permute-start(f32[768,24]{0,1:T(8,128)S(1)} %copy-done.57), channel_id=1, source_target_pairs={{0,13},{1,14},{2,15},{3,16},{4,17},{5,18},{6,19},{7,20},{8,21},{9,... | collective-permute-start | bytes 221192
  3353.7 85.4 %collective-permute-start.11 = (f32[768,24]{0,1:T(8,128)S(1)}, f32[768,24]{0,1:T(8,128)}, u32[]{:S(2)}, u32[]{:S(2)}) collective-permute-start(f32[768,24]{0,1:T(8,128)S(1)} %copy-done.57), channel_id=1, source_target_pairs={{0,12},{1,13},{2,14},{3,15},{4,16},{5,17},{6,18},{7,19},{8,20},{9,... | collective-permute-start | bytes 221192
  3355.7 87.5 %collective-permute-start.10 = (f32[768,24]{0,1:T(8,128)S(1)}, f32[768,24]{0,1:T(8,128)}, u32[]{:S(2)}, u32[]{:S(2)}) collective-permute-start(f32[768,24]{0,1:T(8,128)S(1)} %copy-done.57), channel_id=1, source_target_pairs={{0,11},{1,12},{2,13},{3,14},{4,15},{5,16},{6,17},{7,18},{8,19},{9,... | collective-permute-start | bytes 221192
  3439.2 16.7 collective-permute-start.6
  3443.2 14.8 collective-permute-start.5
  3446.9 62.1 %collective-permute-start.4 = (f32[768,24]{0,1:T(8,128)S(1)}, f32[768,24]{0,1:T(8,128)}, u32[]{:S(2)}, u32[]{:S(2)}) collective-permute-start(f32[768,24]{0,1:T(8,128)S(1)} %copy-done.57), channel_id=1, source_target_pairs={{0,5},{1,6},{2,7},{3,8},{4,9},{5,10},{6,11},{7,12},{8,13},{9,14},{... | collective-permute-start | bytes 221192
  3448.8 60.1 %collective-permute-start.3 = (f32[768,24]{0,1:T(8,128)S(1)}, f32[768,24]{0,1:T(8,128)}, u32[]{:S(2)}, u32[]{:S(2)}) collective-permute-start(f32[768,24]{0,1:T(8,128)S(1)} %copy-done.57), channel_id=1, source_target_pairs={{0,4},{1,5},{2,6},{3,7},{4,8},{5,9},{6,10},{7,11},{8,12},{9,13},{1... | collective-permute-start | bytes 221192
  3450.8 58.2 %collective-permute-start.2 = (f32[768,24]{0,1:T(8,128)S(1)}, f32[768,24]{0,1:T(8,128)}, u32[]{:S(2)}, u32[]{:S(2)}) collective-permute-start(f32[768,24]{0,1:T(8,128)S(1)} %copy-done.57), channel_id=1, source_target_pairs={{0,3},{1,4},{2,5},{3,6},{4,7},{5,8},{6,9},{7,10},{8,11},{9,12},{10... | collective-permute-start | bytes 221192
  3455.9 53.1 %collective-permute-start.1 = (f32[768,24]{0,1:T(8,128)S(1)}, f32[768,24]{0,1:T(8,128)}, u32[]{:S(2)}, u32[]{:S(2)}) collective-permute-start(f32[768,24]{0,1:T(8,128)S(1)} %copy-done.57), channel_id=1, source_target_pairs={{0,2},{1,3},{2,4},{3,5},{4,6},{5,7},{6,8},{7,9},{8,10},{9,11},{10,... | collective-permute-start | bytes 221192
  3458.0 50.9 collective-permute-start
  (328 other events, 41149.9 us)
Sparse Core Ops, SparseCore 0:
  10.3 303.7 all-gather.28
  316.3 303.3 all-gather.20
  622.0 308.8 all-gather.18
  933.0 309.5 all-gather.26
  1244.7 307.6 all-gather.22
  1554.5 309.3 all-gather.24
  1866.2 309.8 all-gather.30
  2178.3 308.9 all-gather.32
  2520.5 659.7 reduce-scatter.18
  3182.6 651.8 reduce-scatter.20
  3836.8 648.3 reduce-scatter.14
  4487.5 648.4 reduce-scatter.16
where the time goes:
time: 5260 us; the launch traced here: 5240 us
  waiting for transfers between devices  3320 us (63%)
  blocking collectives  1140 us (22%)
  starting transfers between devices  336 us (6%)
  local copies, waits for them, and re-layouts  276 us (5%)
  matrix products  109 us (2%)
    reduce_scatter x2, waiting for transfers between devices, reduce_grads(): lax.psum_scatter(expand_grad, ('dp', 'fsdp'), scatter_dimension=1, tiled=...  1300 us
    all_gather x2, blocking collectives, fetch(): lax.all_gather(gains_piece, ('dp', 'fsdp'), axis=1, tiled=True)  617 us
    all_gather x2, waiting for transfers between devices, fetch(): lax.all_gather(shrink_piece, ('dp', 'fsdp'), axis=0, tiled=True)  611 us
    all_gather x2, waiting for transfers between devices, fetch(): lax.all_gather(expand_piece, ('dp', 'fsdp'), axis=1, tiled=True)  576 us
    all_gather x2, waiting for transfers between devices, fetch(): lax.all_gather(joint_piece, ('dp', 'fsdp'), axis=1, tiled=True)  547 us
    unnamed x2, blocking collectives  444 us
    unnamed x128, starting transfers between devices  335 us
    reduce_scatter x2, waiting for transfers between devices, reduce_grads(): lax.psum_scatter(shrink_grad, ('dp', 'fsdp'), scatter_dimension=0, tiled=...  273 us
  transfers between devices with their start and end apart: 140, of which 11 were waited for; matrix products, arithmetic and copies ran while one was open for 14% of the time, Pallas kernels for 0%

commit v1 on v0

v1 whole, which is shorter than its diff:
```python
import jax
import jax.numpy as jnp
from jax import lax
from jax.experimental import pallas as pl
from jax.experimental.pallas import tpu as pltpu
from jax.sharding import PartitionSpec as P

MESH = pl.DeviceIdType.MESH
BF = jnp.bfloat16
F32 = jnp.float32

def place():
    dp = lax.axis_index("dp"); fs = lax.axis_index("fsdp")
    return (dp // 4, lax.rem(dp // 2, 2) * 2 + fs // 4, lax.rem(fs, 4), lax.rem(dp, 2))

def device_at(x, y, z, c):
    return ((x * 2 + y // 2) * 2 + c, lax.rem(y, 2) * 4 + z)

def moved(co, axis, k):
    n = 2 if axis == 3 else 4
    co = list(co)
    co[axis] = lax.rem(co[axis] + (k % n), n)
    return tuple(co)

def greet(co):
    bar = pltpu.get_barrier_semaphore()
    peers = [(a, k) for a in range(3) for k in (1, 2, 3)] + [(3, 1)]
    for a, k in peers:
        pl.semaphore_signal(bar, inc=1, device_id=device_at(*moved(co, a, k)), device_id_type=MESH)
    pl.semaphore_wait(bar, len(peers))

class Link:
    def __init__(self, co, ss, rs):
        self.co, self.ss, self.rs = co, ss, rs
        self.n = 0
        self.out = []
    def send(self, src, dst, axis, k):
        i = self.n
        self.n += 1
        cp = pltpu.make_async_remote_copy(src_ref=src, dst_ref=dst, send_sem=self.ss.at[i], recv_sem=self.rs.at[i],
            device_id=device_at(*moved(self.co, axis, k)), device_id_type=MESH)
        cp.start()
        self.out.append(cp)
        return cp
    def drain(self):
        for cp in self.out:
            cp.wait_send()

class Local:
    def __init__(self, sems):
        self.sems, self.n = sems, 0
    def copy(self, src, dst):
        cp = pltpu.make_async_copy(src, dst, self.sems.at[self.n])
        self.n += 1
        cp.start()
        return cp

class RowSum:
    def __init__(self, link, slots):
        self.link, self.slots, self.n = link, slots, 0

    def send(self, value):
        axis = (2, 1, 0, 3)[self.n]
        mine = self.slots.at[self.n, self.link.co[axis]]
        mine[...] = value
        self.going = [self.link.send(mine, mine, axis, k) for k in ((1, 3, 2) if axis < 3 else (1,))]

    def total(self):
        for cp in self.going:
            cp.wait_recv()
        count = 4 if self.n < 3 else 2
        value = self.slots[self.n, 0]
        for k in range(1, count):
            value = value + self.slots[self.n, k]
        self.n += 1
        return value


def acc(dst, srcs, lead):
    total = 1
    for d in lead:
        total *= d
    def body(t, carry):
        idx = []
        for d in reversed(lead):
            idx.append(lax.rem(t, d))
            t = t // d
        idx = tuple(reversed(idx))
        v = srcs[0][idx].astype(F32)
        for s in srcs[1:]:
            v = v + s[idx].astype(F32)
        dst[idx] = v.astype(dst.dtype)
        return carry
    lax.fori_loop(0, total, body, 0)


D = 768
LAYERS = 2
STEP = 5
beta_first = 0.9
beta_second = 0.999
adam_epsilon = 1e-08
decay_matrix = 0.1
rate_matrix = 0.05
rate_gains = 0.25
clip_limit = 1.0
HEADS = 12
HEAD_DIM = 64
T = 256
norm_epsilon = 1e-05
SQ = 0.7978845608028654
CUBE = 0.044715
highest = lax.Precision.HIGHEST


def dot_of(a, b, dims, **kw):
    return lax.dot_general(a, b, (dims, ((), ())), preferred_element_type=F32, **kw)


def dot_nt(a, b):
    return dot_of(a, b, ((1,), (1,)))


def dot_nn(a, b):
    return dot_of(a, b, ((1,), (0,)))


def dot_tn(a, b):
    return dot_of(a, b, ((0,), (0,)))


def loop(n, fn):
    def body(t, carry):
        fn(t)
        return carry
    lax.fori_loop(0, n, body, 0)


def tile(t, size):
    return pl.ds(pl.multiple_of(t * size, size), size)


def stats(v):
    centred = v - jnp.mean(v, axis=-1, keepdims=True)
    scale = lax.rsqrt(jnp.mean(centred * centred, axis=-1, keepdims=True) + norm_epsilon)
    return centred * scale, scale


def norm_rows(src, dst, gain, shift):
    def step(t):
        r = tile(t, 64)
        unit, _ = stats(src[r, :].astype(F32))
        dst[r, :] = (unit * gain + shift).astype(BF)
    loop(T // 64, step)


def norm_back(src, grad, base, dst, gain, low_dst):
    def step(t, carry):
        to_gain, to_shift = carry
        r = tile(t, 64)
        unit, scale = stats(src[r, :].astype(F32))
        g = grad[r, :]
        to_gain = to_gain + jnp.sum((g * unit).reshape(8, 8, D), axis=0)
        to_shift = to_shift + jnp.sum(g.reshape(8, 8, D), axis=0)
        g = g * gain
        out = base[r, :] + scale * (
            g - jnp.mean(g, axis=-1, keepdims=True) - unit * jnp.mean(g * unit, axis=-1, keepdims=True)
        )
        dst[r, :] = out
        if low_dst is not None:
            low_dst[r, :] = out.astype(BF)
        return (to_gain, to_shift)
    zero = jnp.zeros((8, D), F32)
    to_gain, to_shift = lax.fori_loop(0, T // 64, step, (zero, zero))
    return jnp.sum(to_gain, axis=0, keepdims=True), jnp.sum(to_shift, axis=0, keepdims=True)


def grids():
    return lax.broadcasted_iota(jnp.int32, (T, T), 0), lax.broadcasted_iota(jnp.int32, (T, T), 1)


def halves(pair):
    lane = lax.broadcasted_iota(jnp.int32, (T, 128), 1)
    zero = jnp.zeros_like(pair)
    return jnp.where(lane < HEAD_DIM, pair, zero), jnp.where(lane < HEAD_DIM, zero, pair)


SCALE = HEAD_DIM ** -0.5
FT = 384


def slots_at(ref, t):
    return ref[t // 4, lax.rem(t, 4)].reshape(FT, D)


def put_slots(ref, t, value):
    ref[t // 4, lax.rem(t, 4)] = value.reshape(4, 4, 24, D).astype(BF)


def first_scores(proj):
    q, _ = halves(proj[:, 0:128])
    return dot_nt(q * jnp.asarray(SCALE, BF), proj[:, D:D + 128])


def attention(proj, probs, attended, bias, length):
    row, col = grids()
    scores = first_scores(proj)
    chosen = jnp.maximum(scores, 0.0) + jnp.log(1.0 + jnp.exp(-jnp.abs(scores)))
    chosen = jnp.where((col > 0) & (col < row) & (row < length), chosen, 0.0)
    forget = dot_of((col < row).astype(F32), chosen, ((1,), (0,)), precision=highest)
    bias[...] = jnp.where((col <= row) & (col < length), forget, 1e30)

    def pair(p):
        at = tile(p, 128)
        q = halves(proj[:, at] * jnp.asarray(SCALE, BF))
        k = proj[:, tile(6 + p, 128)]
        v = halves(proj[:, tile(12 + p, 128)])
        total = None
        for h in range(2):
            logits = dot_nt(q[h], k) - bias[...]
            e = jnp.exp(logits - jnp.max(logits, axis=-1, keepdims=True))
            e = (e * (1.0 / jnp.sum(e, axis=-1, keepdims=True))).astype(BF)
            probs[2 * p + h] = e
            part = dot_nn(e, v[h])
            total = part if h == 0 else total + part
        attended[:, at] = total.astype(BF)
    loop(6, pair)


def forward_first(s, gains, length):
    norm_rows(s.stream, s.normed, gains[0:1], gains[1:2])
    s.need("wj")
    wj = s.wj.reshape(3 * D, D)
    def project(t):
        s.proj[:, tile(t, 256)] = dot_nt(s.normed[...], wj[tile(t, 256), :]).astype(BF)
    loop(9, project)
    attention(s.proj, s.probs, s.attended, s.bias, length)
    s.need("wo")
    wo = s.wo.reshape(D, D)
    def output(t):
        at = tile(t, 256)
        s.mid[:, at] = s.stream[:, at].astype(F32) + dot_nt(s.attended[...], wo[at, :])
    loop(3, output)


def forward_second(s, gains):
    norm_rows(s.mid, s.normed2, gains[2:3], gains[3:4])
    s.need("we")
    def raise_(t):
        at = tile(t, FT)
        r = dot_nt(s.normed2[...], slots_at(s.we, t))
        s.raised[:, at] = r
        s.hidden[:, at] = (0.5 * r * (1.0 + jnp.tanh(r * (SQ + SQ * CUBE * r * r)))).astype(BF)
    loop(4 * D // FT, raise_)
    s.need("ws")
    def lower(t):
        at = tile(t, 256)
        s.next[:, at] = s.mid[:, at] + dot_nn(s.hidden[...], s.ws[:, :, :, :, :, at].reshape(4 * D, 256))
    loop(3, lower)


def backward_second(s, gains):
    for name in ("dstream", "ws", "raised", "we", "normed2"):
        s.need(name)
    s.low[...] = s.dstream[...].astype(BF)
    s.acc[...] = jnp.zeros((T, D), F32)
    def step(t):
        at = tile(t, FT)
        dh = dot_nt(s.low[...], slots_at(s.ws, t))
        r = s.raised[:, at]
        th = jnp.tanh(r * (SQ + SQ * CUBE * r * r))
        hid = (0.5 * r * (1.0 + th)).astype(BF)
        slope = 0.5 * (1.0 + th) + 0.5 * r * (1.0 - th * th) * (SQ + 3.0 * SQ * CUBE * r * r)
        dr = (dh * slope).astype(BF)
        put_slots(s.ws, t, dot_tn(hid, s.low[...]))
        s.acc[...] += dot_nn(dr, slots_at(s.we, t))
        put_slots(s.we, t, dot_tn(dr, s.normed2[...]))
    pieces = 4 * D // FT // 2
    for piece in range(pieces):
        loop(2, lambda t: step(t + 2 * piece))
        if piece < pieces - 1:
            yield
    s.need("mid")
    s.sums += norm_back(s.mid, s.acc, s.dstream, s.dstream, gains[2:3], s.low)
    yield


def attention_back(proj, probs, dout, dproj, bias, keep, length):
    bias[...] = jnp.zeros((T, T), F32)

    def scores_of(p, h, do, v):
        prob = probs[2 * p + h]
        full = prob.astype(F32)
        dsoft = dot_nt(do, v)
        dl = full * (dsoft - jnp.sum(full * dsoft, axis=-1, keepdims=True))
        bias[...] += dl
        return prob, dl

    def pair(p):
        at, at_k, at_v = tile(p, 128), tile(6 + p, 128), tile(12 + p, 128)
        q = halves(proj[:, at] * jnp.asarray(SCALE, BF))
        k = halves(proj[:, at_k] * jnp.asarray(SCALE, BF))
        v = proj[:, at_v]
        do = halves(dout[:, at])
        dq = dk = dv = None
        for h in range(2):
            prob, dl = scores_of(p, h, do[h], v)
            ds = dl.astype(BF)
            parts = (dot_nn(ds, k[h]), dot_tn(ds, q[h]), dot_tn(prob, do[h]))
            dq, dk, dv = parts if h == 0 else (dq + parts[0], dk + parts[1], dv + parts[2])
        dproj[:, at] = dq.astype(BF)
        dproj[:, at_k] = dk.astype(BF)
        dproj[:, at_v] = dv.astype(BF)
    loop(2, lambda t: pair(t + 1))
    yield
    loop(3, lambda t: pair(t + 3))
    yield

    q = halves(proj[:, 0:128] * jnp.asarray(SCALE, BF))
    k = halves(proj[:, D:D + 128] * jnp.asarray(SCALE, BF))
    v = proj[:, 2 * D:2 * D + 128]
    do = halves(dout[:, 0:128])
    prob1, dl1 = scores_of(0, 1, do[1], v)
    prob0, dl0 = scores_of(0, 0, do[0], v)
    keep[...] = dl0
    row, col = grids()
    dchosen = -dot_of((col > row).astype(F32), bias[...], ((1,), (0,)), precision=highest)
    scores = first_scores(proj)
    slope = 1.0 / (1.0 + jnp.exp(-scores))
    extra = jnp.where((col > 0) & (col < row) & (row < length), dchosen * slope, 0.0)
    ds0 = (keep[...] + extra).astype(BF)
    ds1 = dl1.astype(BF)
    dproj[:, 0:128] = (dot_nn(ds0, k[0]) + dot_nn(ds1, k[1])).astype(BF)
    dproj[:, D:D + 128] = (dot_tn(ds0, q[0]) + dot_tn(ds1, q[1])).astype(BF)
    dproj[:, 2 * D:2 * D + 128] = (dot_tn(prob0, do[0]) + dot_tn(prob1, do[1])).astype(BF)


def backward_first(s, gains, length):
    for name in ("wo", "attended", "proj", "probs"):
        s.need(name)
    wo, wj = s.wo.reshape(D, D), s.wj.reshape(3 * D, D)
    def back(t):
        at = tile(t, 256)
        s.dout[:, at] = dot_nn(s.low[...], wo[:, at]).astype(BF)
    loop(3, back)
    def grad(t):
        at = tile(t, 256)
        wo[at, :] = dot_tn(s.low[:, at], s.attended[...]).astype(BF)
    loop(3, grad)
    yield
    yield from attention_back(s.proj, s.probs, s.dout, s.dproj, s.bias, s.keep, length)
    yield
    s.need("wj")
    s.need("normed")
    s.acc[...] = jnp.zeros((T, D), F32)
    def joint(t):
        at = tile(t, 256)
        d = s.dproj[:, at]
        s.acc[...] += dot_nn(d, wj[at, :])
        wj[at, :] = dot_tn(d, s.normed[...]).astype(BF)
    for piece in range(3):
        loop(3, lambda t: joint(t + 3 * piece))
        yield
    s.need("stream")
    s.sums += norm_back(s.stream, s.acc, s.dstream, s.dstream, gains[0:1], None)


class Names:
    def __init__(self, **kw):
        self.__dict__.update(kw)
        self.coming = {}
        self.sums = ()

    def need(self, name):
        for cp in self.coming.pop(name, ()):
            cp.wait()


WEIGHTS = dict(wj=((4, 2, 2, 144, D), BF), wo=((4, 2, 2, 48, D), BF), we=((2, 4, 4, 4, 24, D), BF), ws=((2, 4, 4, 4, 24, D), BF))
SAVED = dict(mid=((T, D), F32), normed=((T, D), BF), normed2=((T, D), BF), proj=((T, 3 * D), BF), probs=((HEADS, T, T), BF),
    attended=((T, D), BF), raised=((T, 4 * D), F32))
ONCE = dict(bias=((T, T), F32), hidden=((T, 4 * D), BF), next=((T, D), F32))
BACK = dict(bias=((T, T), F32), keep=((T, T), F32), dstream=((T, D), F32), low=((T, D), BF), acc=((T, D), F32), dout=((T, D), BF),
    dproj=((T, 3 * D), BF))


def fetch(ins, s, loc, names):
    for n in names:
        s.coming[n] = [loc.copy(ins[n], getattr(s, n))]


def run(pieces):
    for _ in pieces:
        pass


def gains_of(sums):
    gain2, shift2, gain1, shift1 = sums
    return jnp.concatenate([gain1, shift1, gain2, shift2], axis=0)


def live_rows(length):
    return lax.broadcasted_iota(jnp.int32, (T, D), 0) < length


def gather_forward_body(ins, out, s, loc, link, co):
    x, y, z, c = co
    lo, hi = pl.ds(0, 2), pl.ds(2, 2)
    W = [[getattr(s, k) for k in WEIGHTS], [out["next_" + k] for k in WEIGHTS]]
    parts = (1, 2, 0)
    first, second, third = (2, 0, 1), (1, 2, 0), (0, 1, 2)
    length = ins["length"][0]
    fetch(ins, s, loc, ("stream",))
    gain_sum = RowSum(link, s.gbuf)
    gain_sum.send(ins["gains"][...])
    own, ph1, ph2, ph2f, ph3, ph3f, sib = {}, {}, {}, {}, {}, {}, {0: [], 1: []}

    def slots(l, part):
        return (s.abuf.at[l], W[l][2].at[c], W[l][3].at[c])[part]

    def start(l):
        for part in parts:
            src = (ins["pa"], ins["pb"], ins["pc"])[part].at[l]
            to = slots(l, part)
            dst = to.at[y, z] if part == 0 else to.at[x, y, z]
            own[l, part] = loc.copy(src, dst)
            ph1[l, part] = [link.send(src, dst, first[part], k) for k in (1, 3, 2)]

    def widen(l):
        for part in parts:
            own[l, part].wait()
            for cp in ph1[l, part]:
                cp.wait_recv()
            to = slots(l, part)
            ref = (lambda: to.at[y], lambda: to.at[:, y, z], lambda: to.at[x, :, z])[part]()
            ph2[l, part] = [link.send(ref, ref, second[part], 1), link.send(ref, ref, second[part], 3)]

    def widen_on(l):
        for part in parts:
            ph2f[l, part] = []
            to = slots(l, part)
            for side, (back, half) in enumerate(((3, lo), (1, hi))):
                ph2[l, part][side].wait_recv()
                q = moved(co, second[part], back)
                ref = (lambda: to.at[q[1], half], lambda: to.at[half, y, q[2]], lambda: to.at[q[0], half, z])[part]()
                ph2f[l, part].append(link.send(ref, ref, second[part], (1, 3)[side]))

    def compact(l):
        for cp in ph2f[l, 0]:
            cp.wait_recv()
        for yy in range(4):
            for zz in range(4):
                v = s.abuf[l, yy, zz].astype(F32)
                at = (yy // 2) * 144 + ((yy % 2) * 4 + zz) * 18
                s.jf[at:at + 18] = v[:18]
                at = (yy // 2) * 48 + ((yy % 2) * 4 + zz) * 6
                s.of[at:at + 6] = v[18:24]
        for h in range(2):
            s.jst[l, h] = s.jf[h * 144:h * 144 + 144].astype(BF)
            s.ost[l, h] = s.of[h * 48:h * 48 + 48].astype(BF)
        mine = [(s.jst.at[l], W[l][0].at[x, :, c]), (s.ost.at[l], W[l][1].at[x, :, c])]
        own[l] = [loc.copy(a, b) for a, b in mine]
        return mine

    def spread(l):
        for part in parts:
            if part == 0:
                pairs = compact(l)
            else:
                for cp in ph2f[l, part]:
                    cp.wait_recv()
                to = slots(l, part)
                ref = to.at[:, y, :] if part == 1 else to.at[:, :, z]
                pairs = [(ref, ref)]
            ph3[l, part] = [[link.send(a, b, third[part], k) for a, b in pairs] for k in (1, 3)]
            sib[l] += [link.send(a, b, 3, 1) for a, b in pairs]

    def pieces(l, part, q, h):
        half = None if h is None else (lo, hi)[h]
        if part == 0:
            at = (q[0], slice(None) if h is None else h, c)
            return [W[l][0].at[at], W[l][1].at[at]]
        to = slots(l, part)
        whole = slice(None) if h is None else half
        return [to.at[whole, q[1], :] if part == 1 else to.at[whole, :, q[2]]]

    def spread_on(l):
        for part in parts:
            ph3f[l, part] = []
            for side, (back, h) in enumerate(((3, 0), (1, 1))):
                for cp in ph3[l, part][side]:
                    cp.wait_recv()
                q = moved(co, third[part], back)
                for ref in pieces(l, part, q, h):
                    ph3f[l, part].append((link.send(ref, ref, third[part], (1, 3)[side]), h))
                for ref in pieces(l, part, q, None):
                    sib[l].append(link.send(ref, ref, 3, 1))

    def finish(l):
        for part in parts:
            q = moved(co, third[part], 2)
            for n, (cp, h) in enumerate(ph3f[l, part]):
                cp.wait_recv()
                refs = pieces(l, part, q, h)
                ref = refs[n % len(refs)]
                sib[l].append(link.send(ref, ref, 3, 1))

    def settle(l):
        for cp in sib[l]:
            cp.wait_recv()
        for cp in own[l]:
            cp.wait()

    start(0)
    start(1)
    widen(0)
    gain_sum.send(gain_sum.total())
    widen(1)
    widen_on(0)
    gain_sum.send(gain_sum.total())
    spread(0)
    widen_on(1)
    gain_sum.send(gain_sum.total())
    spread_on(0)
    out["gains_all"][...] = gain_sum.total()
    spread(1)
    finish(0)
    settle(0)
    done = [loc.copy(getattr(s, k), out[k]) for k in WEIGHTS]
    gains = out["gains_all"][0:4]
    s.need("stream")
    forward_first(s, gains, length)
    done += [loc.copy(getattr(s, k), out[k]) for k in ("normed", "proj", "probs", "attended", "mid")]
    spread_on(1)
    forward_second(s, gains)
    done += [loc.copy(getattr(s, k), out[k]) for k in ("normed2", "raised", "next")]
    finish(1)
    settle(1)
    for cp in done:
        cp.wait()
    link.drain()


def layer1_body(ins, out, s, loc):
    fetch(ins, s, loc, ("stream", "wj", "wo", "we", "ws"))
    n = ins["length"][0]
    g = ins["gains"][4:8]
    s.need("stream")
    forward_first(s, g, n)
    forward_second(s, g)
    out["layer_output"][...] = s.next[...].astype(BF)
    s.dstream[...] = jnp.where(live_rows(n), ins["cotangent"][...].astype(F32), 0.0)
    run(backward_second(s, g))
    done = [loc.copy(s.we, out["we"]), loc.copy(s.ws, out["ws"])]
    run(backward_first(s, g, n))
    done += [loc.copy(s.wj, out["wj"]), loc.copy(s.wo, out["wo"]), loc.copy(s.dstream, out["dstream"])]
    out["gains_grad"][...] = gains_of(s.sums)
    for cp in done:
        cp.wait()


def backward_reduce_body(ins, out, s, loc, link, co):
    x, y, z, c = co
    first, second, third = (0, 1, 2), (1, 2, 0), (2, 0, 1)
    length = ins["length"][0]
    later = [ins["grad_" + k] for k in WEIGHTS]
    here = [getattr(s, k) for k in WEIGHTS]

    def cut(refs, part, q, cc):
        J, O, E, S = refs
        if part == 0:
            return [J.at[q, :, cc], O.at[q, :, cc]]
        return [E.at[cc, :, q]] if part == 1 else [S.at[cc, :, :, q]]

    def own_block(l, part, k):
        if l == 0:
            return cut(here, part, moved(co, first[part], k)[first[part]], c)
        return [r.at[k] for r in ((s.oJ, s.oO), (s.oE,), (s.oS,))[part]]

    def sib_block(part, k):
        return [r.at[k] for r in ((s.sJ, s.sO), (s.sE,), (s.sS,))[part]]

    def buf(name, l, part, side):
        return [getattr(s, name + k).at[l, side] for k in (("J", "O"), ("E",), ("S",))[part]]

    def half(refs, part, h):
        n = 1 if part == 0 else 2
        return [r.at[pl.ds(h * n, n)] for r in refs]

    def add(dsts, srcs, part, halved):
        lead = (1 if halved else 2,) if part == 0 else ((2 if halved else 4), 4)
        for n, d in enumerate(dsts):
            acc(d, [v[n] for v in srcs], lead)

    def send(srcs, dsts, axis, k):
        return [link.send(a, b, axis, k) for a, b in zip(srcs, dsts)]

    def reduce_part(l, p):
        arrive = {}
        for k in (2, 1, 3, 0):
            q = moved(co, first[p], k)[first[p]]
            src = later if l == 1 else here
            mine = [] if l == 0 else [loc.copy(a, b) for a, b in zip(cut(src, p, q, c), own_block(l, p, k))]
            arrive[k] = (mine, send(cut(src, p, q, 1 - c), sib_block(p, k), 3, 1))

        def join(k):
            mine, sibs = arrive[k]
            for cp in mine:
                cp.wait()
            for cp in sibs:
                cp.wait_recv()
            add(own_block(l, p, k), [own_block(l, p, k), sib_block(p, k)], p, False)

        yield
        a = first[p]
        join(2)
        o = own_block(l, p, 2)
        hop1 = (send(half(o, p, 0), buf("r1", l, p, 0), a, 1), send(half(o, p, 1), buf("r1", l, p, 1), a, 3))
        yield
        join(1)
        hop2 = send(half(own_block(l, p, 1), p, 1), half(buf("r2", l, p, 0), p, 1), a, 1)
        join(3)
        hop2 += send(half(own_block(l, p, 3), p, 0), half(buf("r2", l, p, 1), p, 0), a, 3)
        yield
        join(0)
        yield
        for side, k in ((0, 1), (1, 3)):
            for cp in hop1[side]:
                cp.wait_recv()
            o = half(own_block(l, p, k), p, side)
            add(o, [o, buf("r1", l, p, side)], p, True)
            hop2 += send(o, half(buf("r2", l, p, side), p, side), a, k)
        yield
        for cp in hop2:
            cp.wait_recv()
        o, left, right = own_block(l, p, 0), buf("r2", l, p, 0), buf("r2", l, p, 1)
        if p == 0:
            for h in range(2):
                for n, (f, rows) in enumerate(((s.fJ, 144), (s.fO, 48))):
                    f[h * rows:(h + 1) * rows] = o[n][h].astype(F32) + left[n][h].astype(F32) + right[n][h].astype(F32)
            for yy in range(4):
                for zz in range(4):
                    at = (yy // 2) * 144 + ((yy % 2) * 4 + zz) * 18
                    rows = s.fJ[at:at + 18]
                    at = (yy // 2) * 48 + ((yy % 2) * 4 + zz) * 6
                    s.r3[l, yy, zz] = jnp.concatenate([rows, s.fO[at:at + 6]], axis=0).astype(BF)
            block = s.r3.at[l]
        else:
            acc(o[0], [o[0], left[0], right[0]], (4, 4))
            block = o[0]
        ax = second[p]

        def blk(k, h=None):
            q = lax.rem(co[ax] + k, 4)
            part_of = slice(None) if h is None else pl.ds(2 * h, 2)
            return block.at[q, part_of] if p != 1 else block.at[part_of, q]

        hop1 = [link.send(blk(2, 0), s.t1.at[l, p, 0], ax, 1), link.send(blk(2, 1), s.t1.at[l, p, 1], ax, 3)]
        hop2 = [link.send(blk(1, 1), s.t2.at[l, p, 0, pl.ds(2, 2)], ax, 1), link.send(blk(3, 0), s.t2.at[l, p, 1, pl.ds(0, 2)], ax, 3)]
        yield
        for side, k in ((0, 1), (1, 3)):
            hop1[side].wait_recv()
            o = blk(k, side)
            acc(o, [o, s.t1.at[l, p, side]], (2,))
            hop2.append(link.send(o, s.t2.at[l, p, side, pl.ds(2 * side, 2)], ax, k))
        yield
        for cp in hop2:
            cp.wait_recv()
        acc(s.r4.at[l, p], [blk(0), s.t2.at[l, p, 0], s.t2.at[l, p, 1]], (4,))
        ax = third[p]
        me = co[ax]
        last = [link.send(s.r4.at[l, p, lax.rem(me + k, 4)], s.u1.at[l, p, k - 1], ax, k) for k in (1, 3, 2)]
        yield
        for cp in last:
            cp.wait_recv()
        v = s.r4[l, p, me].astype(F32)
        for k in range(3):
            v = v + s.u1[l, p, k].astype(F32)
        out["sum_" + "abc"[p]][l] = v
        yield

    STAGES = 9
    def stages(l, parts, going):
        for _ in range(STAGES - 1):
            for p in parts:
                next(going[l, p])
                yield
        for p in parts:
            run(going[l, p])
            yield

    going = {(l, p): reduce_part(l, p) for l in (1, 0) for p in range(3)}
    sibling = device_at(*moved(co, 3, 1))
    for p in (2, 1, 0):
        next(going[1, p])
    fetch(ins, s, loc, ("dstream", "ws", "raised", "we", "normed2", "mid", "wo", "attended", "proj", "probs", "wj", "normed", "stream"))
    g = ins["gains"][0:4]
    order = (2, 1, 0)
    one = stages(1, order, going)
    steps = [0]
    def advance(n):
        for _ in range(n):
            steps[0] += 1
            next(one, None)
    for _ in backward_second(s, g):
        advance(3)
    advance(max(0, 9 - steps[0]))
    pl.semaphore_signal(s.credit, inc=1, device_id=sibling, device_id_type=MESH)
    pl.semaphore_wait(s.credit, 1)
    next(going[0, 2])
    next(going[0, 1])
    ff = stages(0, (2, 1), going)
    for _ in backward_first(s, g, length):
        if steps[0] < 27:
            advance(3)
        else:
            next(ff, None)
            next(ff, None)
    next(going[0, 0])
    copies = [loc.copy(s.dstream, out["dstream"])]
    gain_sum = RowSum(link, s.gbuf)
    gain_sum.send(jnp.concatenate([gains_of(s.sums), ins["gains_later"][...]], axis=0))
    advance(max(0, 27 - steps[0]))
    joint = stages(0, (0,), going)
    rounds = 0
    while True:
        a, b, d = next(ff, 1), next(ff, 1), next(joint, 1)
        rounds += 1
        if rounds in (2, 4, 6):
            gain_sum.send(gain_sum.total())
        if a and b and d:
            break
    out["gains_sum"][...] = gain_sum.total()
    square = jnp.zeros((24, D), F32)
    for l in range(2):
        for p in range(3):
            v = out["sum_" + "abc"[p]][l]
            square = square + v * v
    part_sum = square[0:8] + square[8:16] + square[16:24]
    piece = part_sum[:, 0:128]
    for n in range(1, 6):
        piece = piece + part_sum[:, n * 128:(n + 1) * 128]
    norm_sum = RowSum(link, s.nbuf)
    for n in range(4):
        norm_sum.send(piece)
        piece = norm_sum.total()
    out["norm"][...] = piece
    for cp in copies:
        cp.wait()
    link.drain()


def call(body, inputs, outs, scratch, copies, remote=0, collective=None, credit=False, limit=60 << 20):
    in_names, out_names, names = list(inputs), list(outs), list(scratch)
    space = {"hbm": pl.ANY, "vmem": pltpu.VMEM, "smem": pltpu.SMEM}
    shapes = [pltpu.VMEM(*scratch[n]) for n in names] + [pltpu.SemaphoreType.DMA((copies,))]
    params = dict(vmem_limit_bytes=limit)
    if remote:
        shapes += [pltpu.SemaphoreType.DMA((remote,)), pltpu.SemaphoreType.DMA((remote,))]
        params.update(collective_id=collective, has_side_effects=True)
    if credit:
        shapes.append(pltpu.SemaphoreType.REGULAR)

    def kernel(*refs):
        ins = dict(zip(in_names, refs))
        out = dict(zip(out_names, refs[len(in_names):]))
        rest = refs[len(in_names) + len(out_names):]
        bufs = Names(**dict(zip(names, rest)))
        loc = Local(rest[len(names)])
        if not remote:
            body(ins, out, bufs, loc)
            return
        if credit:
            bufs.credit = rest[-1]
        co = place()
        greet(co)
        link = Link(co, *rest[len(names) + 1:len(names) + 3])
        body(ins, out, bufs, loc, link, co)

    result = pl.pallas_call(
        kernel,
        out_shape=tuple(jax.ShapeDtypeStruct(*outs[n][1:]) for n in out_names),
        in_specs=[pl.BlockSpec(memory_space=space[inputs[n][0]]) for n in in_names],
        out_specs=tuple(pl.BlockSpec(memory_space=space[outs[n][0]]) for n in out_names),
        scratch_shapes=shapes,
        compiler_params=pltpu.CompilerParams(**params),
    )(*[inputs[n][1] for n in in_names])
    return dict(zip(out_names, result))


def hbm(table, prefix=""):
    return {prefix + k: ("hbm", *v) for k, v in table.items()}


def gather_forward(rows_a, rows_b, rows_c, gains, tokens, length):
    ins = dict(pa=("hbm", rows_a), pb=("hbm", rows_b), pc=("hbm", rows_c), gains=("vmem", gains), stream=("hbm", tokens),
        length=("smem", length))
    outs = {**hbm(WEIGHTS), **hbm(WEIGHTS, "next_"), **hbm(SAVED), "next": ("hbm", (T, D), F32), "gains_all": ("vmem", (8, D), F32)}
    own = dict(stream=((T, D), BF), abuf=((2, 4, 4, 24, D), BF), jf=((288, D), F32), of=((96, D), F32), jst=((2, 2, 144, D), BF),
        ost=((2, 2, 48, D), BF), gbuf=((4, 4, 8, D), F32))
    return call(gather_forward_body, ins, outs, {**WEIGHTS, **SAVED, **ONCE, **own}, 40, remote=144, collective=0)


def layer1(stream, length, cotangent, weights, gains):
    ins = dict(stream=("hbm", stream), length=("smem", length), cotangent=("vmem", cotangent), gains=("vmem", gains),
        **{k: ("hbm", w) for k, w in weights.items()})
    outs = dict(layer_output=("vmem", (T, D), BF), dstream=("hbm", (T, D), F32), gains_grad=("vmem", (4, D), F32), **hbm(WEIGHTS))
    return call(layer1_body, ins, outs, {**WEIGHTS, **SAVED, **ONCE, **BACK, "stream": ((T, D), F32)}, 16)


def backward_reduce(tokens, length, dstream, weights, gains, saved, grads, gains_later):
    ins = dict(stream=("hbm", tokens), length=("smem", length), dstream=("hbm", dstream), gains=("vmem", gains),
        gains_later=("vmem", gains_later), **{k: ("hbm", w) for k, w in weights.items()}, **{k: ("hbm", saved[k]) for k in SAVED},
        **{"grad_" + k: ("hbm", w) for k, w in grads.items()})
    rows = ("vmem", (2, 24, D), F32)
    outs = dict(dstream=("hbm", (T, D), F32), sum_a=rows, sum_b=rows, sum_c=rows, gains_sum=("vmem", (8, D), F32),
        norm=("vmem", (8, 128), F32))
    own = {}
    for k, a, b in (("J", (2, 144), None), ("O", (2, 48), None), ("E", (4, 4, 24), None), ("S", (4, 4, 24), None)):
        halved = (a[0] // 2, *a[1:])
        own["o" + k] = ((4, *a, D), BF)
        own["s" + k] = ((4, *a, D), BF)
        own["r1" + k] = ((2, 2, *halved, D), BF)
        own["r2" + k] = ((2, 2, *a, D), BF)
    own.update(fJ=((288, D), F32), fO=((96, D), F32), r3=((2, 4, 4, 24, D), BF), t1=((2, 3, 2, 2, 24, D), BF),
        t2=((2, 3, 2, 4, 24, D), BF), r4=((2, 3, 4, 24, D), BF), u1=((2, 3, 3, 24, D), BF), gbuf=((4, 4, 8, D), F32),
        nbuf=((4, 4, 8, 128), F32))
    return call(backward_reduce_body, ins, outs, {**WEIGHTS, **SAVED, **BACK, "stream": ((T, D), BF), **own}, 40, remote=176,
        collective=1, credit=True)


def adam_update(master, gradient, moment, square, rate, decay, clip_factor):
    clipped = gradient * clip_factor
    momentum = beta_first * moment + (1.0 - beta_first) * clipped
    variance = beta_second * square + (1.0 - beta_second) * clipped * clipped
    corrected_first = momentum / (1.0 - beta_first**STEP)
    corrected_second = variance / (1.0 - beta_second**STEP)
    updated = master - rate * (
        corrected_first / (jnp.sqrt(corrected_second) + adam_epsilon) + decay * master
    )
    return (updated, momentum, variance)


def local(
    tokens,
    lengths,
    cotangent,
    joint_weight,
    output_weight,
    expand_weight,
    shrink_weight,
    layer_gains,
    joint_moment,
    output_moment,
    expand_moment,
    shrink_moment,
    gains_moment,
    joint_square,
    output_square,
    expand_square,
    shrink_square,
    gains_square,
):
    swap = lambda a: a.transpose(0, 2, 1)
    rows_a = jnp.concatenate([swap(joint_weight), swap(output_weight)], axis=1).astype(BF)
    which_device = lax.axis_index("dp") * 8 + lax.axis_index("fsdp")
    gains_rows = lax.dynamic_update_slice(
        jnp.zeros((8, D), F32), layer_gains.astype(BF).astype(F32).reshape(8, 6), (0, which_device * 6)
    )
    ahead = gather_forward(rows_a, swap(expand_weight).astype(BF), shrink_weight.astype(BF), gains_rows, tokens, lengths)
    gains = ahead["gains_all"]
    top = layer1(ahead["next"], lengths, cotangent, {k: ahead["next_" + k] for k in WEIGHTS}, gains)
    back = backward_reduce(tokens, lengths, top["dstream"], {k: ahead[k] for k in WEIGHTS}, gains, ahead,
        {k: top[k] for k in WEIGHTS}, top["gains_grad"])
    layer_output, dstream = top["layer_output"], back["dstream"]
    gains_sum, sum_a = back["gains_sum"], back["sum_a"]
    gains_own = lax.dynamic_slice(gains_sum, (0, which_device * 6), (8, 6)).reshape(LAYERS, 4, 6)
    stacked = [swap(sum_a[:, :18]), swap(sum_a[:, 18:]), swap(back["sum_b"]), back["sum_c"], gains_own]
    total_square = jnp.sum(back["norm"]) + jnp.sum(gains_sum * gains_sum)
    gradient_norm = jnp.sqrt(total_square)
    clip_factor = jnp.minimum(1.0, clip_limit / (gradient_norm + 1e-06))
    joint_new = adam_update(
        joint_weight, stacked[0], joint_moment, joint_square, rate_matrix, decay_matrix, clip_factor
    )
    output_new = adam_update(
        output_weight,
        stacked[1],
        output_moment,
        output_square,
        rate_matrix,
        decay_matrix,
        clip_factor,
    )
    expand_new = adam_update(
        expand_weight,
        stacked[2],
        expand_moment,
        expand_square,
        rate_matrix,
        decay_matrix,
        clip_factor,
    )
    shrink_new = adam_update(
        shrink_weight,
        stacked[3],
        shrink_moment,
        shrink_square,
        rate_matrix,
        decay_matrix,
        clip_factor,
    )
    gains_new = adam_update(
        layer_gains, stacked[4], gains_moment, gains_square, rate_gains, 0.0, clip_factor
    )
    return (
        layer_output,
        dstream,
        gradient_norm,
        joint_new[0],
        output_new[0],
        expand_new[0],
        shrink_new[0],
        gains_new[0],
        joint_new[1],
        output_new[1],
        expand_new[1],
        shrink_new[1],
        gains_new[1],
        joint_new[2],
        output_new[2],
        expand_new[2],
        shrink_new[2],
        gains_new[2],
    )


def solution(mesh):
    in_specs = (
        P(("dp", "fsdp"), None),
        P(("dp", "fsdp")),
        P(("dp", "fsdp"), None),
        P(None, None, ("dp", "fsdp")),
        P(None, None, ("dp", "fsdp")),
        P(None, None, ("dp", "fsdp")),
        P(None, ("dp", "fsdp"), None),
        P(None, None, ("dp", "fsdp")),
        P(None, None, ("dp", "fsdp")),
        P(None, None, ("dp", "fsdp")),
        P(None, None, ("dp", "fsdp")),
        P(None, ("dp", "fsdp"), None),
        P(None, None, ("dp", "fsdp")),
        P(None, None, ("dp", "fsdp")),
        P(None, None, ("dp", "fsdp")),
        P(None, None, ("dp", "fsdp")),
        P(None, ("dp", "fsdp"), None),
        P(None, None, ("dp", "fsdp")),
    )
    out_specs = (
        P(("dp", "fsdp"), None),
        P(("dp", "fsdp"), None),
        P(),
        P(None, None, ("dp", "fsdp")),
        P(None, None, ("dp", "fsdp")),
        P(None, None, ("dp", "fsdp")),
        P(None, ("dp", "fsdp"), None),
        P(None, None, ("dp", "fsdp")),
        P(None, None, ("dp", "fsdp")),
        P(None, None, ("dp", "fsdp")),
        P(None, None, ("dp", "fsdp")),
        P(None, ("dp", "fsdp"), None),
        P(None, None, ("dp", "fsdp")),
        P(None, None, ("dp", "fsdp")),
        P(None, None, ("dp", "fsdp")),
        P(None, None, ("dp", "fsdp")),
        P(None, ("dp", "fsdp"), None),
        P(None, None, ("dp", "fsdp")),
    )
    return jax.shard_map(local, mesh=mesh, in_specs=in_specs, out_specs=out_specs, check_vma=False)
```

time: 5260 us -> 252 us (0.05)
  waiting for transfers between devices: 3320 us -> 0 us
  blocking collectives: 1140 us -> 0 us
  starting transfers between devices: 336 us -> 0 us
  local copies, waits for them, and re-layouts: 276 us -> 5.32 us
  Pallas kernels: 0 us -> 227 us
  matrix products: 109 us -> 0 us
    all_gather x8 -> x0, waiting for transfers between devices: 1730 us -> none  [the longest x2 611 us: fetch(): lax.all_gather(shrink_piece, ('dp', 'fsdp'), axis=0, tiled=True)]
    reduce_scatter x4 -> x0, waiting for transfers between devices: 1570 us -> none  [the longest x2 1300 us: reduce_grads(): lax.psum_scatter(expand_grad, ('dp', 'fsdp'), scatter_dimension=1, tiled=...]
    all_gather x2 -> x0, blocking collectives: 617 us -> none  [fetch(): lax.all_gather(gains_piece, ('dp', 'fsdp'), axis=1, tiled=True)]
    unnamed x2 -> x0, blocking collectives: 444 us -> none
    unnamed x128 -> x0, starting transfers between devices: 335 us -> none
    pallas_call x0 -> x3, Pallas kernels: none -> 227 us  [call(): pl.pallas_call(kernel, out_shape=tuple((jax.ShapeDtypeStruct(*outs[n][1:]...]
    unnamed x519 -> x41, local copies, waits for them, and re-layouts: 191 us -> 4.99 us
    dot_general x40 -> x0, matrix products: 109 us -> none  [the longest x2 14.1 us: layer_backward(): jnp.einsum('tf,td->fd', hidden, dbranch, preferred_element_type=jnp.float32)]
  transfers between devices with their start and end apart: 140 -> 0, of which waited for: 11 -> 0; matrix products, arithmetic and copies ran while one was open for 14% -> 0% of each run, Pallas kernels for 0% -> 0%
where the time goes in v1:
time: 252 us
  Pallas kernels  227 us (90%)
  other arithmetic  15.7 us (6%)
  local copies, waits for them, and re-layouts  5.32 us (2%)
  between operations  4.03 us (2%)
    pallas_call x3, Pallas kernels, call(): pl.pallas_call(kernel, out_shape=tuple((jax.ShapeDtypeStruct(*outs[n][1:]...  227 us
    sub x5, other arithmetic, adam_update(): master - rate * (corrected_first / (jnp.sqrt(corrected_second) + adam_eps...  6.01 us

profile of v1, /device:TPU:1, one launch (start us, length us, event | category | flops | bytes accessed | tf_op | source)
XLA Modules:
  0.0 251.6 jit_solution(15999691251535519436)
XLA Ops:
  1.3 0.7 convert_element_type.16
  2.0 0.8 convert.10
  2.8 0.3 dynamic_update_slice.3.refs_3_
  3.1 0.0 copy-start.11
  3.1 0.9 convert.9
  4.1 0.6 pad_maximum_fusion.refs_0_
  4.8 1.6 convert_bitcast_fusion.refs_1_
  6.3 1.6 convert_element_type.15.refs_2_
  7.9 0.0 copy-done.11
  7.9 73.5 %shard_map.313 = (bf16[4,2,2,144,768]{4,3,2,1,0:T(8,128)(2,1)}, bf16[4,2,2,48,768]{4,3,2,1,0:T(8,128)(2,1)}, bf16[2,4,4,4,24,768]{5,4,3,2,1,0:T(8,128)(2,1)}, bf...) custom-call(bf16[2,24,768]{2,1,0:T(8,128)(2,1)} %pad_maximum_fusion., ...), custom_call_target="tpu_custom_call" | custom-call | tf_op jit(solution)/shard_map/pallas_call | solution.py:780
  81.3 40.1 %shard_map.314 = (bf16[256,768]{1,0:T(8,128)(2,1)}, f32[256,768]{1,0:T(8,128)}, f32[4,768]{1,0:T(4,128)}, bf16[4,2,2,144,768]{4,3,2,1,0:T(8,128)(2,1)}, bf16[4,2...) custom-call(f32[256,768]{1,0:T(8,128)} %get-tuple-element.48.refs_0_, ...), custom_call_target="tpu_custom_call" | custom-call | tf_op jit(solution)/shard_map/pallas_call | solution.py:780
  121.4 0.0 copy-start.14
  121.5 0.0 copy-start.15
  121.5 0.0 copy-start.16
  121.5 0.0 copy-start.8
  121.5 0.0 copy-start.12
  121.5 0.0 copy-start.13
  121.5 0.0 copy-start.1
  121.5 0.0 copy-start.4
  121.5 0.0 copy-start.5
  121.6 0.0 copy-start.2
  121.6 0.0 copy-start.6
  121.6 0.0 copy-start.7
  121.6 0.0 copy-start.3
  121.6 0.0 copy-start.9
  121.6 0.0 copy-start.10
  121.6 113.0 %shard_map.315 = (f32[256,768]{1,0:T(8,128)}, f32[2,24,768]{2,1,0:T(8,128)}, f32[2,24,768]{2,1,0:T(8,128)}, f32[2,24,768]{2,1,0:T(8,128)}, f32[8,768]{1,0:T(8,128)}, /*index=5*/f32[8,128]{1,0:T(8,128)}) custom-call(bf16[256,768]{1,0:T(8,128)(2,1)} %refs_0_.1, s32[1]{0:T(128)S(6)} %copy.106.refs_5_.refs_1_, f32[256,768]{1,0:T(8,128)} %get-tuple-element.55.refs_2_, ...), custom_call_target="tpu_custom_call" | custom-call | tf_op jit(solution)/shard_map/pallas_call | solution.py:780
  234.6 0.0 copy-start
  234.6 1.4 multiply_reduce_fusion
  236.0 1.3 reduce_sum.18
  238.7 0.8 dynamic-slice_multiply_fusion
  239.5 0.0 copy-done.14
  239.5 0.0 copy-done.15
  239.5 0.0 copy-done.16
  239.5 0.6 multiply_subtract_fusion.2
  240.1 0.0 copy-done.8
  240.1 0.0 copy-done.12
  240.1 0.0 copy-done.13
  240.1 0.9 copy_subtract_fusion.1
  241.0 0.6 copy.63
  241.6 0.6 copy.65
  242.3 0.6 copy.67
  242.9 0.0 copy-done.1
  242.9 0.0 copy-done.4
  242.9 0.0 copy-done.5
  242.9 1.7 multiply_subtract_fusion
  244.7 0.0 copy-done.2
  244.7 0.0 copy-done.6
  244.7 0.0 copy-done.7
  244.7 1.7 multiply_subtract_fusion.1
  246.4 0.0 copy-done.3
  246.4 0.0 copy-done.9
  246.4 0.0 copy-done.10
  246.4 1.0 copy_subtract_fusion
  247.5 0.7 copy.62
  248.2 0.7 copy.64
  248.9 0.7 copy.66
  249.6 0.0 copy-done
  249.6 0.9 copy.107
  (4 shorter events, 0.0 us)
Async XLA Ops:
  3.1 4.7 %copy-start.11 = (f32[8,768]{1,0:T(8,128)}, f32[8,768]{1,0:T(8,128)S(1)}, u32[]{:S(2)}) copy-start(f32[8,768]{1,0:T(8,128)S(1)} %dynamic_update_slice.3.refs_3_) | copy-start | bytes 73732
  121.4 118.1 %copy-start.14 = (f32[2,4,6]{2,1,0:T(4,128)S(1)}, f32[2,4,6]{2,1,0:T(4,128)}, u32[]{:S(2)}) copy-start(f32[2,4,6]{2,1,0:T(4,128)} %param.25) | copy-start | bytes 580
  121.5 118.0 %copy-start.15 = (f32[2,4,6]{2,1,0:T(4,128)S(1)}, f32[2,4,6]{2,1,0:T(4,128)}, u32[]{:S(2)}) copy-start(f32[2,4,6]{2,1,0:T(4,128)} %param.30) | copy-start | bytes 580
  121.5 118.0 %copy-start.16 = (f32[2,4,6]{2,1,0:T(4,128)S(1)}, f32[2,4,6]{2,1,0:T(4,128)}, u32[]{:S(2)}) copy-start(f32[2,4,6]{2,1,0:T(4,128)} %param.35) | copy-start | bytes 580
  121.5 118.6 %copy-start.8 = (f32[2,768,6]{1,0,2:T(2,128)S(1)}, f32[2,768,6]{1,0,2:T(2,128)}, u32[]{:S(2)}) copy-start(f32[2,768,6]{1,0,2:T(2,128)} %param.22) | copy-start | bytes 110596
  121.5 118.6 %copy-start.12 = (f32[2,768,6]{1,0,2:T(2,128)S(1)}, f32[2,768,6]{1,0,2:T(2,128)}, u32[]{:S(2)}) copy-start(f32[2,768,6]{1,0,2:T(2,128)} %param.27) | copy-start | bytes 110596
  121.5 118.6 %copy-start.13 = (f32[2,768,6]{1,0,2:T(2,128)S(1)}, f32[2,768,6]{1,0,2:T(2,128)}, u32[]{:S(2)}) copy-start(f32[2,768,6]{1,0,2:T(2,128)} %param.32) | copy-start | bytes 110596
  121.5 121.4 %copy-start.1 = (f32[2,24,768]{2,1,0:T(8,128)S(1)}, f32[2,24,768]{2,1,0:T(8,128)}, u32[]{:S(2)}) copy-start(f32[2,24,768]{2,1,0:T(8,128)} %param.24) | copy-start | bytes 442372
  121.5 121.4 %copy-start.4 = (f32[2,24,768]{2,1,0:T(8,128)S(1)}, f32[2,24,768]{2,1,0:T(8,128)}, u32[]{:S(2)}) copy-start(f32[2,24,768]{2,1,0:T(8,128)} %param.29) | copy-start | bytes 442372
  121.5 121.4 %copy-start.5 = (f32[2,24,768]{2,1,0:T(8,128)S(1)}, f32[2,24,768]{2,1,0:T(8,128)}, u32[]{:S(2)}) copy-start(f32[2,24,768]{2,1,0:T(8,128)} %param.34) | copy-start | bytes 442372
  121.6 123.1 %copy-start.2 = (f32[2,768,24]{1,2,0:T(8,128)S(1)}, f32[2,768,24]{1,2,0:T(8,128)}, u32[]{:S(2)}) copy-start(f32[2,768,24]{1,2,0:T(8,128)} %param.23) | copy-start | bytes 442372
  121.6 123.1 %copy-start.6 = (f32[2,768,24]{1,2,0:T(8,128)S(1)}, f32[2,768,24]{1,2,0:T(8,128)}, u32[]{:S(2)}) copy-start(f32[2,768,24]{1,2,0:T(8,128)} %param.28) | copy-start | bytes 442372
  121.6 123.1 %copy-start.7 = (f32[2,768,24]{1,2,0:T(8,128)S(1)}, f32[2,768,24]{1,2,0:T(8,128)}, u32[]{:S(2)}) copy-start(f32[2,768,24]{1,2,0:T(8,128)} %param.33) | copy-start | bytes 442372
  121.6 124.8 %copy-start.3 = (f32[2,768,18]{1,0,2:T(2,128)S(1)}, f32[2,768,18]{1,0,2:T(2,128)}, u32[]{:S(2)}) copy-start(f32[2,768,18]{1,0,2:T(2,128)} %param.21) | copy-start | bytes 331780
  121.6 124.8 %copy-start.9 = (f32[2,768,18]{1,0,2:T(2,128)S(1)}, f32[2,768,18]{1,0,2:T(2,128)}, u32[]{:S(2)}) copy-start(f32[2,768,18]{1,0,2:T(2,128)} %param.26) | copy-start | bytes 331780
  121.6 124.8 %copy-start.10 = (f32[2,768,18]{1,0,2:T(2,128)S(1)}, f32[2,768,18]{1,0,2:T(2,128)}, u32[]{:S(2)}) copy-start(f32[2,768,18]{1,0,2:T(2,128)} %param.31) | copy-start | bytes 331780
  234.6 15.0 %copy-start = (f32[256,768]{1,0:T(8,128)S(1)}, f32[256,768]{1,0:T(8,128)}, u32[]{:S(2)}) copy-start(f32[256,768]{1,0:T(8,128)} %get-tuple-element.148) | copy-start | bytes 2359300

commit v2 on v1

v2 whole, which is shorter than its diff:
```python
import jax
import jax.numpy as jnp
import numpy as np
from jax import lax
from jax.experimental import pallas as pl
from jax.experimental.pallas import tpu as pltpu
from jax.sharding import PartitionSpec as P

MESH = pl.DeviceIdType.MESH
BF = jnp.bfloat16
F32 = jnp.float32
ANY, VMEM, SMEM = pl.ANY, pltpu.VMEM, pltpu.SMEM

def place():
    dp = lax.axis_index("dp"); fs = lax.axis_index("fsdp")
    return (dp // 4, lax.rem(dp // 2, 2) * 2 + fs // 4, lax.rem(fs, 4), lax.rem(dp, 2))

def device_at(x, y, z, c):
    return ((x * 2 + y // 2) * 2 + c, lax.rem(y, 2) * 4 + z)

def moved(co, axis, k):
    n = 2 if axis == 3 else 4
    co = list(co)
    co[axis] = lax.rem(co[axis] + (k % n), n)
    return tuple(co)

PLANES = ((1, 2), (0, 2), (0, 1))
RINGS = ((1, 2), (2, 0), (0, 1))
CORNERS = [(a, b) for a in range(4) for b in range(4) if (a, b) != (0, 0)]


def greet(co, planes):
    steps = {(0, 0, k, 1) for k in range(4)}
    for k in (1, 2, 3):
        steps |= {(k, 0, 0, 0), (0, k, 0, 0), (0, 0, k, 0)}
    for axes in planes:
        for corner in CORNERS:
            step = [0, 0, 0, 0]
            step[axes[0]], step[axes[1]] = corner
            steps.add(tuple(step))
    bar = pltpu.get_barrier_semaphore()
    for step in sorted(steps):
        pl.semaphore_signal(bar, inc=1, device_id=device_at(*stepped(co, step)), device_id_type=MESH)
    return lambda: pl.semaphore_wait(bar, len(steps))


def stepped(co, step):
    for axis, k in enumerate(step):
        if k:
            co = moved(co, axis, k)
    return co


class Link:
    def __init__(self, co, ss, rs):
        self.co, self.ss, self.rs = co, ss, rs
        self.n = 0
        self.out = []
    def send(self, src, dst, axis, k):
        i = self.n
        self.n += 1
        cp = pltpu.make_async_remote_copy(src_ref=src, dst_ref=dst, send_sem=self.ss.at[i], recv_sem=self.rs.at[i],
            device_id=device_at(*moved(self.co, axis, k)), device_id_type=MESH)
        cp.start()
        self.out.append(cp)
        return cp
    def step(self, src, dst, step):
        i = self.n
        self.n += 1
        cp = pltpu.make_async_remote_copy(src_ref=src, dst_ref=dst, send_sem=self.ss.at[i], recv_sem=self.rs.at[i],
            device_id=device_at(*stepped(self.co, step)), device_id_type=MESH)
        cp.start()
        self.out.append(cp)
        return cp

    def plane(self, axes, src_of, dst_of):
        going = []
        for a, b in CORNERS:
            step = [0, 0, 0, 0]
            step[axes[0]], step[axes[1]] = a, b
            going.append(self.step(src_of(a, b), dst_of(a, b), step))
        return going

    def plane_at_once(self, axes, src_of, landing):
        i = self.n
        self.n += 1
        for n, (a, b) in enumerate(CORNERS):
            step = [0, 0, 0, 0]
            step[axes[0]], step[axes[1]] = a, b
            pltpu.make_async_remote_copy(src_ref=src_of(a, b), dst_ref=landing.at[n], send_sem=self.ss.at[i], recv_sem=self.rs.at[i],
                device_id=device_at(*stepped(self.co, step)), device_id_type=MESH).start()
        whole = pltpu.make_async_remote_copy(src_ref=landing, dst_ref=landing, send_sem=self.ss.at[i], recv_sem=self.rs.at[i],
            device_id=device_at(*moved(self.co, 3, 1)), device_id_type=MESH)
        self.out.append(whole)
        return whole

    def sent(self, copies):
        for cp in copies:
            cp.wait_send()
        self.out = [o for o in self.out if all(o is not cp for cp in copies)]

    def drain(self):
        for cp in self.out:
            cp.wait_send()

class Local:
    def __init__(self, sems):
        self.sems, self.n = sems, 0
    def copy(self, src, dst):
        cp = pltpu.make_async_copy(src, dst, self.sems.at[self.n])
        self.n += 1
        cp.start()
        return cp

class WideSum:
    def __init__(self, link, wide, deep):
        self.link, self.wide, self.deep = link, wide, deep

    def first(self, value):
        x, y, z, c = self.link.co
        mine = self.wide.at[x, y]
        mine[...] = value
        self.going = self.link.plane((0, 1), lambda a, b: mine, lambda a, b: mine)

    def second(self):
        x, y, z, c = self.link.co
        for cp in self.going:
            cp.wait_recv()
        value = None
        for i in range(4):
            for j in range(4):
                v = self.wide[i, j]
                value = v if value is None else value + v
        mine = self.deep.at[z, c]
        mine[...] = value
        self.going = [self.link.step(mine, mine, (0, 0, a, b)) for a in range(4) for b in range(2) if a or b]

    def total(self):
        for cp in self.going:
            cp.wait_recv()
        value = None
        for i in range(4):
            for j in range(2):
                v = self.deep[i, j]
                value = v if value is None else value + v
        return value


def acc(dst, srcs, lead):
    lead = lead[:-1]
    total = 1
    for d in lead:
        total *= d

    def body(t, carry):
        idx = []
        for d in reversed(lead):
            idx.append(lax.rem(t, d))
            t = t // d
        idx = tuple(reversed(idx))
        v = srcs[0][idx].astype(F32)
        for src in srcs[1:]:
            v = v + src[idx].astype(F32)
        dst[idx] = v.astype(dst.dtype)
        return carry

    lax.fori_loop(0, total, body, 0)


D = 768
LAYERS = 2
STEP = 5
beta_first = 0.9
beta_second = 0.999
adam_epsilon = 1e-08
clip_limit = 1.0
HEADS = 12
HEAD_DIM = 64
T = 256
norm_epsilon = 1e-05
SQ = 0.7978845608028654
CUBE = 0.044715
highest = lax.Precision.HIGHEST


def dot_of(a, b, dims, **kw):
    return lax.dot_general(a, b, (dims, ((), ())), preferred_element_type=F32, **kw)


def dot_nt(a, b):
    return dot_of(a, b, ((1,), (1,)))


def dot_nn(a, b):
    return dot_of(a, b, ((1,), (0,)))


def dot_tn(a, b):
    return dot_of(a, b, ((0,), (0,)))


def loop(n, fn):
    def body(t, carry):
        fn(t)
        return carry
    lax.fori_loop(0, n, body, 0)


def tile(t, size):
    return pl.ds(pl.multiple_of(t * size, size), size)


def stats(v):
    centred = v - jnp.mean(v, axis=-1, keepdims=True)
    scale = lax.rsqrt(jnp.mean(centred * centred, axis=-1, keepdims=True) + norm_epsilon)
    return centred * scale, scale


def norm_rows(src, dst, gain, shift):
    def step(t):
        r = tile(t, 64)
        unit, _ = stats(src[r, :].astype(F32))
        dst[r, :] = (unit * gain + shift).astype(BF)
    loop(T // 64, step)


def norm_back(src, grad, base, dst, gain, low_dst):
    def step(t, carry):
        to_gain, to_shift = carry
        r = tile(t, 64)
        unit, scale = stats(src[r, :].astype(F32))
        g = grad[r, :]
        to_gain = to_gain + jnp.sum((g * unit).reshape(8, 8, D), axis=0)
        to_shift = to_shift + jnp.sum(g.reshape(8, 8, D), axis=0)
        g = g * gain
        out = base[r, :] + scale * (
            g - jnp.mean(g, axis=-1, keepdims=True) - unit * jnp.mean(g * unit, axis=-1, keepdims=True)
        )
        dst[r, :] = out
        if low_dst is not None:
            low_dst[r, :] = out.astype(BF)
        return (to_gain, to_shift)
    zero = jnp.zeros((8, D), F32)
    to_gain, to_shift = lax.fori_loop(0, T // 64, step, (zero, zero))
    return jnp.sum(to_gain, axis=0, keepdims=True), jnp.sum(to_shift, axis=0, keepdims=True)


def grids():
    return lax.broadcasted_iota(jnp.int32, (T, T), 0), lax.broadcasted_iota(jnp.int32, (T, T), 1)


def halves(pair):
    lane = lax.broadcasted_iota(jnp.int32, (T, 128), 1)
    zero = jnp.zeros_like(pair)
    return jnp.where(lane < HEAD_DIM, pair, zero), jnp.where(lane < HEAD_DIM, zero, pair)


SCALE = HEAD_DIM ** -0.5
FT = 384


def slots_at(ref, t, f):
    return ref[t, f // 4, lax.rem(f, 4)].reshape(FT, 256)


def put_slots(ref, f, value):
    for t in range(3):
        ref[t, f // 4, lax.rem(f, 4)] = value[:, 256 * t:256 * t + 256].reshape(4, 4, 24, 256).astype(BF)


def first_scores(proj):
    q, _ = halves(proj[:, 0:128])
    return dot_nt(q * jnp.asarray(SCALE, BF), proj[:, D:D + 128])


def attention(proj, probs, attended, bias, length):
    row, col = grids()
    scores = first_scores(proj)
    chosen = jnp.maximum(scores, 0.0) + jnp.log(1.0 + jnp.exp(-jnp.abs(scores)))
    chosen = jnp.where((col > 0) & (col < row) & (row < length), chosen, 0.0)
    forget = dot_of((col < row).astype(F32), chosen, ((1,), (0,)), precision=highest)
    bias[...] = jnp.where((col <= row) & (col < length), forget, 1e30)

    def pair(p):
        at = tile(p, 128)
        q = halves(proj[:, at] * jnp.asarray(SCALE, BF))
        k = proj[:, tile(6 + p, 128)]
        v = halves(proj[:, tile(12 + p, 128)])
        total = None
        for h in range(2):
            logits = dot_nt(q[h], k) - bias[...]
            e = jnp.exp(logits - jnp.max(logits, axis=-1, keepdims=True))
            e = (e * (1.0 / jnp.sum(e, axis=-1, keepdims=True))).astype(BF)
            probs[2 * p + h] = e
            part = dot_nn(e, v[h])
            total = part if h == 0 else total + part
        attended[:, at] = total.astype(BF)
    loop(6, pair)


def forward_first(s, gains, length):
    norm_rows(s.stream, s.normed, gains[0:1], gains[1:2])
    wj = s.wj.reshape(3 * D, D)
    def project(t):
        s.proj[:, tile(t, 256)] = dot_nt(s.normed[...], wj[tile(t, 256), :]).astype(BF)
    loop(9, project)
    yield
    attention(s.proj, s.probs, s.attended, s.bias, length)
    yield
    wo = s.wo.reshape(D, D)
    def output(t):
        at = tile(t, 256)
        s.mid[:, at] = s.stream[:, at].astype(F32) + dot_nt(s.attended[...], wo[at, :])
    loop(3, output)


def third(t):
    return slice(256 * t, 256 * t + 256)


def forward_second(s, gains):
    norm_rows(s.mid, s.normed2, gains[2:3], gains[3:4])
    s.need("we")
    def raise_(f):
        at = tile(f, FT)
        r = dot_nt(s.normed2[:, third(0)], slots_at(s.we, 0, f))
        for t in (1, 2):
            r = r + dot_nt(s.normed2[:, third(t)], slots_at(s.we, t, f))
        s.raised[:, at] = r
        s.hidden[:, at] = (0.5 * r * (1.0 + jnp.tanh(r * (SQ + SQ * CUBE * r * r)))).astype(BF)
    loop(4 * D // FT, raise_)
    yield
    s.need("ws")
    for t in range(3):
        s.next[:, third(t)] = s.mid[:, third(t)] + dot_nn(s.hidden[...], s.ws[t].reshape(4 * D, 256))


def backward_second(s, gains):
    for name in ("dstream", "ws", "raised", "we", "normed2"):
        s.need(name)
    s.low[...] = s.dstream[...].astype(BF)
    s.acc[...] = jnp.zeros((T, D), F32)
    def step(t):
        at = tile(t, FT)
        dh = dot_nt(s.low[:, third(0)], slots_at(s.ws, 0, t))
        for n in (1, 2):
            dh = dh + dot_nt(s.low[:, third(n)], slots_at(s.ws, n, t))
        r = s.raised[:, at]
        th = jnp.tanh(r * (SQ + SQ * CUBE * r * r))
        hid = (0.5 * r * (1.0 + th)).astype(BF)
        slope = 0.5 * (1.0 + th) + 0.5 * r * (1.0 - th * th) * (SQ + 3.0 * SQ * CUBE * r * r)
        dr = (dh * slope).astype(BF)
        put_slots(s.ws, t, dot_tn(hid, s.low[...]))
        for n in range(3):
            s.acc[:, third(n)] += dot_nn(dr, slots_at(s.we, n, t))
        put_slots(s.we, t, dot_tn(dr, s.normed2[...]))
    pieces = 4 * D // FT // 2
    for piece in range(pieces):
        loop(2, lambda t: step(t + 2 * piece))
        if piece < pieces - 1:
            yield
    s.need("mid")
    s.sums += norm_back(s.mid, s.acc, s.dstream, s.dstream, gains[2:3], s.low)
    yield


def attention_back(proj, probs, dout, dproj, bias, keep, length):
    bias[...] = jnp.zeros((T, T), F32)

    def scores_of(p, h, do, v):
        prob = probs[2 * p + h]
        full = prob.astype(F32)
        dsoft = dot_nt(do, v)
        dl = full * (dsoft - jnp.sum(full * dsoft, axis=-1, keepdims=True))
        bias[...] += dl
        return prob, dl

    def pair(p):
        at, at_k, at_v = tile(p, 128), tile(6 + p, 128), tile(12 + p, 128)
        q = halves(proj[:, at] * jnp.asarray(SCALE, BF))
        k = halves(proj[:, at_k] * jnp.asarray(SCALE, BF))
        v = proj[:, at_v]
        do = halves(dout[:, at])
        dq = dk = dv = None
        for h in range(2):
            prob, dl = scores_of(p, h, do[h], v)
            ds = dl.astype(BF)
            parts = (dot_nn(ds, k[h]), dot_tn(ds, q[h]), dot_tn(prob, do[h]))
            dq, dk, dv = parts if h == 0 else (dq + parts[0], dk + parts[1], dv + parts[2])
        dproj[:, at] = dq.astype(BF)
        dproj[:, at_k] = dk.astype(BF)
        dproj[:, at_v] = dv.astype(BF)
    loop(2, lambda t: pair(t + 1))
    yield
    loop(3, lambda t: pair(t + 3))
    yield

    q = halves(proj[:, 0:128] * jnp.asarray(SCALE, BF))
    k = halves(proj[:, D:D + 128] * jnp.asarray(SCALE, BF))
    v = proj[:, 2 * D:2 * D + 128]
    do = halves(dout[:, 0:128])
    prob1, dl1 = scores_of(0, 1, do[1], v)
    prob0, dl0 = scores_of(0, 0, do[0], v)
    keep[...] = dl0
    row, col = grids()
    dchosen = -dot_of((col > row).astype(F32), bias[...], ((1,), (0,)), precision=highest)
    scores = first_scores(proj)
    slope = 1.0 / (1.0 + jnp.exp(-scores))
    extra = jnp.where((col > 0) & (col < row) & (row < length), dchosen * slope, 0.0)
    ds0 = (keep[...] + extra).astype(BF)
    ds1 = dl1.astype(BF)
    dproj[:, 0:128] = (dot_nn(ds0, k[0]) + dot_nn(ds1, k[1])).astype(BF)
    dproj[:, D:D + 128] = (dot_tn(ds0, q[0]) + dot_tn(ds1, q[1])).astype(BF)
    dproj[:, 2 * D:2 * D + 128] = (dot_tn(prob0, do[0]) + dot_tn(prob1, do[1])).astype(BF)


def backward_first(s, gains, length):
    for name in ("wo", "attended", "proj", "probs"):
        s.need(name)
    wo, wj = s.wo.reshape(D, D), s.wj.reshape(3 * D, D)
    def back(t):
        at = tile(t, 256)
        s.dout[:, at] = dot_nn(s.low[...], wo[:, at]).astype(BF)
    loop(3, back)
    def grad(t):
        at = tile(t, 256)
        wo[at, :] = dot_tn(s.low[:, at], s.attended[...]).astype(BF)
    loop(3, grad)
    yield
    yield from attention_back(s.proj, s.probs, s.dout, s.dproj, s.bias, s.keep, length)
    yield
    s.need("wj")
    s.need("normed")
    s.acc[...] = jnp.zeros((T, D), F32)
    def joint(t):
        at = tile(t, 384)
        d = s.dproj[:, at]
        s.acc[...] += dot_nn(d, wj[at, :])
        wj[at, :] = dot_tn(d, s.normed[...]).astype(BF)
    for piece in range(2):
        loop(3, lambda t: joint(t + 3 * piece))
        yield
    s.need("stream")
    s.sums += norm_back(s.stream, s.acc, s.dstream, s.dstream, gains[0:1], None)


class Names:
    def __init__(self, **kw):
        self.__dict__.update(kw)
        self.coming = {}
        self.sums = ()

    def need(self, name):
        for cp in self.coming.pop(name, ()):
            cp.wait()


WEIGHTS = dict(wj=((4, 2, 2, 144, D), BF), wo=((4, 2, 2, 48, D), BF), we=((3, 2, 4, 4, 4, 24, 256), BF), ws=((3, 2, 4, 4, 4, 24, 256), BF))
SAVED = dict(mid=((T, D), F32), normed=((T, D), BF), normed2=((T, D), BF), proj=((T, 3 * D), BF), probs=((HEADS, T, T), BF),
    attended=((T, D), BF), raised=((T, 4 * D), F32))
ONCE = dict(bias=((T, T), F32), hidden=((T, 4 * D), BF), next=((T, D), F32))
BACK = dict(bias=((T, T), F32), keep=((T, T), F32), dstream=((T, D), F32), low=((T, D), BF), acc=((T, D), F32), dout=((T, D), BF),
    dproj=((T, 3 * D), BF))


def fetch(ins, s, loc, names):
    for n in names:
        s.coming[n] = [loc.copy(getattr(ins, n), getattr(s, n))]


def run(pieces):
    for _ in pieces:
        pass


def gains_of(sums):
    gain2, shift2, gain1, shift1 = sums
    return jnp.concatenate([gain1, shift1, gain2, shift2], axis=0)


def live_rows(length):
    return lax.broadcasted_iota(jnp.int32, (T, D), 0) < length


def own_columns(which):
    lane = lax.broadcasted_iota(jnp.int32, (1, D), 1)
    return [(lane == which * 6 + j).astype(F32) for j in range(6)]


OWN = ((3, 4, 4, 4, 24, 256), BF)
SIBLING = dict(sib_wj=((4, 2, 144, D), BF), sib_wo=((4, 2, 48, D), BF), sib_we=OWN, sib_ws=OWN)


def side_of(ref, name, core, at=slice(None)):
    return ref.at[at, :, core] if name in ("wj", "wo") else ref.at[:, core]


class Pair:
    def __init__(self, s, link, c):
        self.s, self.link, self.c = s, link, c
        self.going, self.copies = {}, {}

    def send(self, name, at=slice(None)):
        src, dst = side_of(getattr(self.s, name), name, 1 - self.c, at), getattr(self.s, "sib_" + name)
        cp = self.link.send(src, dst.at[at] if name == "wj" else dst, 3, 1)
        self.going.setdefault(name, []).append(cp)
        self.copies.setdefault(name, []).append(cp)

    def arrived(self, name):
        for cp in self.going.pop(name):
            cp.wait_recv()

    def join(self, name):
        self.arrived(name)
        mine, other = side_of(getattr(self.s, name), name, self.c), getattr(self.s, "sib_" + name)
        acc(mine, [mine, other], (3, 4, 4))

    def join_rows(self, perm):
        self.arrived("wj")
        self.arrived("wo")
        s = self.s
        def step(n):
            x, h = n // 2, lax.rem(n, 2)
            j = s.wj[x, h, self.c].astype(F32) + s.sib_wj[x, h].astype(F32)
            o = s.wo[x, h, self.c].astype(F32) + s.sib_wo[x, h].astype(F32)
            rows = jnp.concatenate([j.astype(BF), o.astype(BF)], axis=0)
            slots = dot_tn(perm, rows)
            for t in range(3):
                s.ga[t, x, pl.ds(2 * h, 2)] = slots[:, 256 * t:256 * t + 256].reshape(2, 4, 24, 256).astype(BF)
        loop(8, step)


def compact(slots, wj, wo, perm):
    def step(n):
        x, h, c = n // 4, lax.rem(n // 2, 2), lax.rem(n, 2)
        for t in range(3):
            rows = dot_nn(perm, slots[t, c, x, pl.ds(2 * h, 2)].reshape(192, 256)).astype(BF)
            wj[x, h, c, :, third(t)] = rows[:144]
            wo[x, h, c, :, third(t)] = rows[144:]
    loop(16, step)


class Gather:
    def __init__(self, link, loc, piece, dst):
        self.link, self.loc, self.piece, self.dst = link, loc, piece, dst
        self.co = link.co

    def slots(self, t, sel):
        return self.dst.at[(t, self.co[3], *sel)]

    def small(self):
        self.own, self.one = [], []
        for t in range(3):
            src, dst = self.piece.at[:, third(t)], self.slots(t, self.co[:3])
            self.own.append(self.loc.copy(src, dst))
            self.one.append([self.link.send(src, dst, RINGS[t][0], k) for k in (1, 3, 2)])

    def slab(self):
        self.two = []
        for t in range(3):
            self.own[t].wait()
            for cp in self.one[t]:
                cp.wait_recv()
            u, v = RINGS[t]
            sel = list(self.co[:3])
            sel[u] = slice(None)
            ref = self.slots(t, sel)
            self.two.append([self.link.send(ref, ref, v, k) for k in (1, 3)])

    def slab_on(self):
        self.three = []
        for t in range(3):
            u, v = RINGS[t]
            for side, back, on in ((0, 3, 1), (1, 1, 3)):
                self.two[t][side].wait_recv()
                sel = list(moved(self.co, v, back)[:3])
                sel[u] = pl.ds(2 * side, 2)
                ref = self.slots(t, sel)
                self.three.append(self.link.send(ref, ref, v, on))

    def block(self):
        for cp in self.three:
            cp.wait_recv()
        self.four = []
        for t in range(3):
            sel = [slice(None)] * 3
            sel[t] = self.co[t]
            ref = self.slots(t, sel)
            self.four.append([self.link.send(ref, ref, t, k) for k in (1, 3)])

    def block_on(self):
        self.five = []
        for t in range(3):
            u, v = RINGS[t]
            for side, back, on in ((0, 3, 1), (1, 1, 3)):
                self.four[t][side].wait_recv()
                sel = [slice(None)] * 3
                sel[t] = moved(self.co, t, back)[t]
                sel[u] = pl.ds(2 * side, 2)
                ref = self.slots(t, sel)
                self.five.append(self.link.send(ref, ref, t, on))

    def across(self):
        for cp in self.five:
            cp.wait_recv()
        c = self.co[3]
        self.six = [self.link.send(self.dst.at[t, c], self.dst.at[t, c], 3, 1) for t in range(3)]

    def sent(self):
        groups = (*self.one, *self.two, self.three, *self.four, self.five, self.six)
        self.link.sent([cp for g in groups for cp in g])

    def ready(self):
        for cp in self.six:
            cp.wait_recv()


def first_body(ins, out, s, loc, link, co):
    x, y, z, c = co
    length = ins.length[0]
    fetch(ins, s, loc, ("stream",))
    targets = [[s.slots.at[0], s.we, s.ws], [s.slots.at[1], out.top_we, out.top_ws]]
    items = []
    for l in range(2):
        rows = jnp.concatenate([ins.joint[:, l, :], ins.output[:, l, :]], axis=0)
        for w, value in enumerate((rows, ins.expand[l], ins.shrink[l])):
            s.piece[l, w] = value.astype(BF)
            items.append(Gather(link, loc, s.piece.at[l, w], targets[l][w]))
    s.met()
    for item in items:
        item.small()
    which = ((x * 2 + y // 2) * 2 + c) * 8 + lax.rem(y, 2) * 4 + z
    masks = own_columns(which)
    placed = []
    for l in range(2):
        rows = ins.layer_gains[l].astype(BF).astype(F32)
        total = rows[:, 0:1] * masks[0]
        for j in range(1, 6):
            total = total + rows[:, j:j + 1] * masks[j]
        placed.append(total)
    gain_sum = WideSum(link, s.gwide, s.gdeep)
    gain_sum.first(jnp.concatenate(placed, axis=0))

    done = []
    perm = ins.perm

    def step(k):
        if k + 2 < 6:
            items[k + 2].block()
        if 0 < k < 7:
            items[k - 1].across()
        if k < 6:
            items[k].block_on()

    def save(*names, prefix=""):
        for n in names:
            done.append(loc.copy(getattr(s, n), getattr(out, prefix + n)))

    for name in ("slab", "slab_on"):
        for item in items:
            getattr(item, name)()
        if name == "slab":
            gain_sum.second()
    items[0].block()
    items[1].block()
    out.gains_all[...] = gain_sum.total()
    gains = out.gains_all[0:4]
    step(0)
    step(1)
    items[0].ready()
    compact(s.slots.at[0], s.wj, s.wo, perm[...])
    step(2)
    save("wj", "wo")
    s.need("stream")
    first = forward_first(s, gains, length)
    next(first)
    next(first)
    step(3)
    run(first)
    items[1].ready()
    second = forward_second(s, gains)
    next(second)
    step(4)
    items[2].ready()
    save("normed", "proj", "probs", "attended", "mid", "normed2", "raised")
    run(second)
    s.second[...] = s.next[...]
    for cp in done:
        cp.wait()
    done.clear()
    save("we", "ws")
    done.append(loc.copy(s.second, out.top_stream))
    top = Names(**{k: v for k, v in s.__dict__.items() if k not in ("coming", "sums", "stream", "met")}, stream=s.second)
    gains = out.gains_all[4:8]
    items[3].ready()
    compact(s.slots.at[1], s.wj, s.wo, perm[...])
    save("wj", "wo", prefix="top_")
    step(5)
    first = forward_first(top, gains, length)
    next(first)
    step(6)
    items[4].ready()
    items[1].sent()
    for cp in done:
        cp.wait()
    done.clear()
    top.coming["we"] = [loc.copy(out.top_we, s.we)]
    next(first)
    run(first)
    save("normed", "proj", "probs", "attended", "mid", prefix="top_")
    second = forward_second(top, gains)
    next(second)
    save("normed2", "raised", prefix="top_")
    items[5].ready()
    items[2].sent()
    top.coming["ws"] = [loc.copy(out.top_ws, s.ws)]
    run(second)
    out.layer_output[...] = s.next[...].astype(BF)
    for cp in done:
        cp.wait()
    link.drain()


class Reduce:
    def __init__(self, link, s, l, w, source):
        self.link, self.s, self.l, self.w, self.source, self.co = link, s, l, w, source, link.co

    def at(self, t, k):
        sel = [slice(None)] * 3
        sel[t] = moved(self.co, t, k)[t]
        return self.source.at[(t, *sel)]

    def half(self, ref, h):
        return ref.at[pl.ds(2 * h, 2)]

    def r1(self, t, side):
        return self.s.r1.at[self.l, self.w, t, side]

    def r2(self, t, side):
        return self.s.r2.at[self.l, t, side, :, :, self.w]

    def far(self):
        self.hop1 = [[self.link.send(self.half(self.at(t, 2), side), self.r1(t, side), t, k) for side, k in ((0, 1), (1, 3))]
            for t in range(3)]

    def near(self):
        self.hop2 = [[self.link.send(self.half(self.at(t, k), 1 - side), self.half(self.r2(t, side), 1 - side), t, k)
            for side, k in ((0, 1), (1, 3))] for t in range(3)]

    def onward(self):
        for t in range(3):
            for side, k in ((0, 1), (1, 3)):
                self.hop1[t][side].wait_recv()
                o = self.half(self.at(t, k), side)
                acc(o, [o, self.r1(t, side)], (2, 4))
                self.hop2[t].append(self.link.send(o, self.half(self.r2(t, side), side), t, k))

    def collect(self):
        for t in range(3):
            for cp in self.hop2[t]:
                cp.wait_recv()
            acc(self.r2(t, 0), [self.at(t, 0), self.r2(t, 0), self.r2(t, 1)], (4, 4))

    def sent(self):
        self.link.sent([cp for t in range(3) for cp in (*self.hop1[t], *self.hop2[t])])


class Settle:
    def __init__(self, link, s, l, first, count):
        self.link, self.s, self.l, self.first, self.count = link, s, l, first, count
        self.which = pl.ds(first, count)

    def send(self):
        co, self.going = self.link.co, []
        for t in range(3):
            u, v = PLANES[t]
            block = self.s.r2.at[self.l, t, 0]
            pick = lambda a, b: block.at[lax.rem(co[u] + a, 4), lax.rem(co[v] + b, 4), self.which]
            self.going.append(self.link.plane_at_once(PLANES[t], pick, self.s.u1.at[self.l, t, :, self.which]))

    def final(self, square):
        co = self.link.co
        for t in range(3):
            u, v = PLANES[t]
            self.going[t].wait_recv()
            for w in range(self.first, self.first + self.count):
                g = self.s.r2[self.l, t, 0, co[u], co[v], w].astype(F32)
                for k in range(15):
                    g = g + self.s.u1[self.l, t, k, w].astype(F32)
                self.s.grads[self.l, w, :, third(t)] = g
                g = g * g
                g = g[0:8] + g[8:16] + g[16:24]
                g = g[:, 0:128] + g[:, 128:256]
                square = g if square is None else square + g
        return square


def second_body(ins, out, s, loc, link, co):
    x, y, z, c = co
    length = ins.length[0]
    shared = {k: v for k, v in s.__dict__.items() if k not in ("coming", "sums", "met")}
    base = Names(**shared)
    top = Names(**{**shared, **{k: getattr(s, "top_" + k) for k in ("we", "ws", "stream")}})
    layers = (base, top)
    pairs = [Pair(n, link, c) for n in layers]
    sums = [[Reduce(link, s, l, w, (n.ga, n.we.at[:, c], n.ws.at[:, c])[w]) for w in range(3)] for l, n in enumerate(layers)]
    low, up = sums
    top_end, ff_end, row_end = Settle(link, s, 1, 0, 3), Settle(link, s, 0, 1, 2), Settle(link, s, 0, 0, 1)
    perm = ins.perm

    def bring(n, prefix, *names):
        for name in names:
            n.coming[name] = [loc.copy(getattr(ins, prefix + name), getattr(n, name))]

    bring(top, "top_", "ws", "raised", "we", "normed2", "mid", "wo", "attended", "proj", "probs", "wj", "normed", "stream")
    bring(base, "", "we", "ws", "stream")
    s.dstream[...] = jnp.where(live_rows(length), ins.cotangent[...].astype(F32), 0.0)
    g = ins.gains[4:8]
    run(backward_second(top, g))
    s.met()
    pairs[1].send("ws")
    bring(base, "", "raised", "normed2", "mid")
    for k, _ in enumerate(backward_first(top, g, length)):
        if k == 0:
            pairs[1].send("we")
            pairs[1].send("wo")
        if k == 1:
            pairs[1].join("ws")
            up[2].far()
            up[2].near()
        if k == 2:
            pairs[1].join("we")
            up[1].far()
            up[1].near()
        if k == 3:
            bring(base, "", "attended", "proj", "probs")
        if k == 4:
            pairs[1].send("wj", pl.ds(0, 2))
            up[2].onward()
        if k == 5:
            pairs[1].send("wj", pl.ds(2, 2))
    up[1].onward()
    bring(base, "", "normed")
    square = None
    base.coming["dstream"] = []
    g = ins.gains[0:4]
    for k, _ in enumerate(backward_second(base, g)):
        if k == 0:
            pairs[1].join_rows(perm[...])
            up[0].far()
            up[0].near()
            link.sent(pairs[1].copies["wj"] + pairs[1].copies["wo"])
            bring(base, "", "wj", "wo")
            pl.semaphore_signal(s.credit, inc=1, device_id=device_at(*moved(co, 3, 1)), device_id_type=MESH)
            up[2].collect()
        if k == 1:
            up[1].collect()
        if k == 2:
            up[0].onward()
    pl.semaphore_wait(s.credit, 1)
    pairs[0].send("ws")
    for k, _ in enumerate(backward_first(base, g, length)):
        if k == 0:
            pairs[0].send("we")
            pairs[0].send("wo")
            up[0].collect()
            top_end.send()
        if k == 1:
            pairs[0].join("ws")
            low[2].far()
            low[2].near()
        if k == 2:
            pairs[0].join("we")
            low[1].far()
            low[1].near()
        if k == 3:
            square = top_end.final(square)
            up[0].sent()
        if k == 4:
            pairs[0].send("wj", pl.ds(0, 2))
            low[2].onward()
        if k == 5:
            pairs[0].send("wj", pl.ds(2, 2))
            low[1].onward()
    gain_sum = WideSum(link, s.gwide, s.gdeep)
    gain_sum.first(jnp.concatenate([gains_of(base.sums), gains_of(top.sums)], axis=0))
    copies = [loc.copy(s.dstream, out.dstream)]
    low[2].collect()
    pairs[0].join_rows(perm[...])
    low[0].far()
    low[0].near()
    low[1].collect()
    ff_end.send()
    low[0].onward()
    gain_sum.second()
    square = ff_end.final(square)
    low[0].collect()
    row_end.send()
    gains_sum = gain_sum.total()
    out.gains_sum[...] = gains_sum
    square = row_end.final(square)
    copies.append(loc.copy(s.grads, out.grads))
    norm_sum = WideSum(link, s.nwide, s.ndeep)
    norm_sum.first(square)
    norm_sum.second()
    whole = norm_sum.total()
    norm = jnp.sqrt(jnp.sum(jnp.sum(whole, axis=0, keepdims=True), axis=1, keepdims=True)
        + jnp.sum(jnp.sum(gains_sum * gains_sum, axis=0, keepdims=True), axis=1, keepdims=True))
    out.norm[...] = jnp.broadcast_to(norm, (8, 128))
    for cp in copies:
        cp.wait()
    link.drain()


RATES = dict(matrix=(0.05, 0.1), gains=(0.25, 0.0))


def adam(master, gradient, moment, square, kind, clip):
    rate, decay = RATES[kind]
    clipped = gradient * clip
    momentum = beta_first * moment + (1.0 - beta_first) * clipped
    variance = beta_second * square + (1.0 - beta_second) * clipped * clipped
    corrected_first = momentum / (1.0 - beta_first**STEP)
    corrected_second = variance / (1.0 - beta_second**STEP)
    updated = master - rate * (corrected_first / (jnp.sqrt(corrected_second) + adam_epsilon) + decay * master)
    return updated, momentum, variance


def update_body(ins, out, s, loc, link, co):
    x, y, z, c = co
    out.input_gradient[...] = ins.dstream[...]
    out.layer_output[...] = ins.low_output[...]
    which = ((x * 2 + y // 2) * 2 + c) * 8 + lax.rem(y, 2) * 4 + z
    columns = [jnp.sum(ins.gains_sum[...] * m, axis=-1, keepdims=True) for m in own_columns(which)]
    lane = lax.broadcasted_iota(jnp.int32, (8, 6), 1)
    own_gains = jnp.zeros((8, 6), F32)
    for j in range(6):
        own_gains = own_gains + jnp.where(lane == j, columns[j], 0.0)
    norm = ins.norm[0:1, 0:1]
    out.gradient_norm[...] = norm
    clip = jnp.minimum(1.0, clip_limit / (norm + 1e-06))
    for l in range(2):
        for name, w, rows in (("joint", 0, slice(0, 18)), ("output", 0, slice(18, 24)), ("expand", 1, slice(0, 24)), ("shrink", 2, slice(0, 24))):
            at = (slice(None), l, slice(None)) if w == 0 else (l, slice(None), slice(None))
            new = adam(getattr(ins, name)[at], ins.grads[l, w, rows, :], getattr(ins, name + "_moment")[at], getattr(ins, name + "_square")[at], "matrix", clip)
            for kind, v in zip(("master", "momentum", "variance"), new):
                getattr(out, name + "_" + kind)[at] = v
        new = adam(ins.layer_gains[l], own_gains[4 * l:4 * l + 4], ins.gains_moment[l], ins.gains_square[l], "gains", clip)
        for kind, v in zip(("master", "momentum", "variance"), new):
            getattr(out, "gains_" + kind)[l] = v


def call(body, inputs, outs, scratch, copies, remote=0, collective=None, planes=(), credit=False, limit=63 << 20):
    in_names, out_names, names = list(inputs), list(outs), list(scratch)
    shapes = [pltpu.VMEM(*scratch[n]) for n in names] + [pltpu.SemaphoreType.DMA((copies,))]
    params = dict(vmem_limit_bytes=limit)
    if remote:
        shapes += [pltpu.SemaphoreType.DMA((remote,)), pltpu.SemaphoreType.DMA((remote,))]
        params.update(collective_id=collective, has_side_effects=True)
    if credit:
        shapes.append(pltpu.SemaphoreType.REGULAR)

    def kernel(*refs):
        ins = Names(**dict(zip(in_names, refs)))
        out = Names(**dict(zip(out_names, refs[len(in_names):])))
        rest = refs[len(in_names) + len(out_names):]
        bufs = Names(**dict(zip(names, rest)))
        loc = Local(rest[len(names)])
        co = place()
        if not remote:
            body(ins, out, bufs, loc, None, co)
            return
        if credit:
            bufs.credit = rest[-1]
        bufs.met = greet(co, planes)
        link = Link(co, *rest[len(names) + 1:len(names) + 3])
        body(ins, out, bufs, loc, link, co)

    result = pl.pallas_call(
        kernel,
        out_shape=tuple(jax.ShapeDtypeStruct(*outs[n][1:]) for n in out_names),
        in_specs=[pl.BlockSpec(memory_space=inputs[n][0]) for n in in_names],
        out_specs=tuple(pl.BlockSpec(memory_space=outs[n][0]) for n in out_names),
        scratch_shapes=shapes,
        compiler_params=pltpu.CompilerParams(**params),
    )(*[inputs[n][1] for n in in_names])
    return Names(**dict(zip(out_names, result)))


def hbm(table, prefix=""):
    return {prefix + k: (ANY, *v) for k, v in table.items()}


ROWS = dict(joint=((18, 2, D), F32), output=((6, 2, D), F32), expand=((2, 24, D), F32), shrink=((2, 24, D), F32))
SUMS = dict(gwide=((4, 4, 8, D), F32), gdeep=((4, 2, 8, D), F32))


def slot_order():
    order = np.zeros((192, 192), np.float32)
    for f in range(8):
        for r in range(18):
            order[18 * f + r, 24 * f + r] = 1
        for r in range(6):
            order[144 + 6 * f + r, 24 * f + 18 + r] = 1
    return jnp.asarray(order, BF)


def first_kernel(shards, layer_gains, tokens, length, perm):
    ins = dict(layer_gains=(VMEM, layer_gains), stream=(ANY, tokens), length=(SMEM, length), perm=(VMEM, perm),
        **{k: (VMEM, v) for k, v in shards.items()})
    row = ((T, D), F32)
    outs = {**hbm(WEIGHTS), **hbm(SAVED), **hbm(WEIGHTS, "top_"), **hbm(SAVED, "top_"), "top_stream": (ANY, *row),
        "gains_all": (VMEM, (8, D), F32), "layer_output": (VMEM, (T, D), BF)}
    own = dict(stream=((T, D), BF), second=row, piece=((2, 3, 24, D), BF), slots=((2, 3, 2, 4, 4, 4, 24, 256), BF))
    return call(first_body, ins, outs, {**WEIGHTS, **SAVED, **ONCE, **own, **SUMS}, 64, 272, 0, ((0, 1),))


def second_kernel(tokens, length, cotangent, ahead, perm):
    names = (*WEIGHTS, *SAVED)
    ins = dict(stream=(ANY, tokens), length=(SMEM, length), perm=(VMEM, perm), cotangent=(VMEM, cotangent),
        gains=(VMEM, ahead.gains_all), top_stream=(ANY, ahead.top_stream), **{k: (ANY, getattr(ahead, k)) for k in names},
        **{"top_" + k: (ANY, getattr(ahead, "top_" + k)) for k in names})
    outs = dict(dstream=(ANY, (T, D), F32), norm=(VMEM, (8, 128), F32), grads=(ANY, (2, 3, 24, D), F32),
        gains_sum=(VMEM, (8, D), F32))
    own = dict(stream=((T, D), BF), top_stream=((T, D), F32), ga=OWN, r1=((2, 3, 3, 2, 2, 4, 24, 256), BF),
        r2=((2, 3, 2, 4, 4, 3, 24, 256), BF), u1=((2, 3, 15, 3, 24, 256), BF), grads=((2, 3, 24, D), F32),
        nwide=((4, 4, 8, 128), F32), ndeep=((4, 2, 8, 128), F32))
    weights = {"top_" + k: WEIGHTS[k] for k in ("we", "ws")}
    return call(second_body, ins, outs, {**WEIGHTS, **weights, **SAVED, **BACK, **own, **SUMS, **SIBLING}, 64, 200, 1, PLANES,
        credit=True)


def update(state, ahead, back):
    ins = dict(dstream=(VMEM, back.dstream), low_output=(VMEM, ahead.layer_output), norm=(VMEM, back.norm),
        grads=(VMEM, back.grads), gains_sum=(VMEM, back.gains_sum), **{k: (VMEM, v) for k, v in state.items()})
    outs = dict(input_gradient=(VMEM, (T, D), F32), layer_output=(VMEM, (T, D), BF), gradient_norm=(VMEM, (1, 1), F32))
    for kind in ("master", "momentum", "variance"):
        for name, v in {**ROWS, "gains": ((2, 4, 6), F32)}.items():
            outs[name + "_" + kind] = (VMEM, *v)
    return call(update_body, ins, outs, {}, 1)


def local(
    tokens,
    lengths,
    cotangent,
    joint_weight,
    output_weight,
    expand_weight,
    shrink_weight,
    layer_gains,
    joint_moment,
    output_moment,
    expand_moment,
    shrink_moment,
    gains_moment,
    joint_square,
    output_square,
    expand_square,
    shrink_square,
    gains_square,
):
    front = lambda a: a.transpose(2, 0, 1)
    swap = lambda a: a.transpose(0, 2, 1)
    shards = dict(joint=front(joint_weight), output=front(output_weight), expand=swap(expand_weight), shrink=shrink_weight)
    perm = slot_order()
    ahead = first_kernel(shards, layer_gains, tokens, lengths, perm)
    back = second_kernel(tokens, lengths, cotangent, ahead, perm)
    state = dict(
        shards,
        joint_moment=front(joint_moment),
        output_moment=front(output_moment),
        expand_moment=swap(expand_moment),
        shrink_moment=shrink_moment,
        joint_square=front(joint_square),
        output_square=front(output_square),
        expand_square=swap(expand_square),
        shrink_square=shrink_square,
        layer_gains=layer_gains,
        gains_moment=gains_moment,
        gains_square=gains_square,
    )
    new = update(state, ahead, back)
    results = [new.layer_output, new.input_gradient, new.gradient_norm.reshape(())]
    for kind in ("master", "momentum", "variance"):
        results += [
            getattr(new, "joint_" + kind).transpose(1, 2, 0),
            getattr(new, "output_" + kind).transpose(1, 2, 0),
            swap(getattr(new, "expand_" + kind)),
            getattr(new, "shrink_" + kind),
            getattr(new, "gains_" + kind),
        ]
    return tuple(results)


AXES = ("dp", "fsdp")


def solution(mesh):
    in_specs = (
        P(AXES, None),
        P(AXES),
        P(AXES, None),
        P(None, None, AXES),
        P(None, None, AXES),
        P(None, None, AXES),
        P(None, AXES, None),
        P(None, None, AXES),
        P(None, None, AXES),
        P(None, None, AXES),
        P(None, None, AXES),
        P(None, AXES, None),
        P(None, None, AXES),
        P(None, None, AXES),
        P(None, None, AXES),
        P(None, None, AXES),
        P(None, AXES, None),
        P(None, None, AXES),
    )
    out_specs = (
        P(AXES, None),
        P(AXES, None),
        P(),
        P(None, None, AXES),
        P(None, None, AXES),
        P(None, None, AXES),
        P(None, AXES, None),
        P(None, None, AXES),
        P(None, None, AXES),
        P(None, None, AXES),
        P(None, None, AXES),
        P(None, AXES, None),
        P(None, None, AXES),
        P(None, None, AXES),
        P(None, None, AXES),
        P(None, None, AXES),
        P(None, AXES, None),
        P(None, None, AXES),
    )
    return jax.shard_map(local, mesh=mesh, in_specs=in_specs, out_specs=out_specs, check_vma=False)
```

time: 252 us -> 220 us (0.87)
  other arithmetic: 15.7 us -> 0 us
  Pallas kernels: 227 us -> 218 us
  local copies, waits for them, and re-layouts: 5.32 us -> 0 us
  between operations: 4.03 us -> 1.5 us
    pallas_call x3, Pallas kernels: 227 us -> 218 us  [call(): pl.pallas_call(kernel, out_shape=tuple((jax.ShapeDtypeStruct(*outs[n][1:]...]
    sub x5 -> x0, other arithmetic: 6.01 us -> none  [adam_update(): master - rate * (corrected_first / (jnp.sqrt(corrected_second) + adam_eps...]
    unnamed x41 -> x0, local copies, waits for them, and re-layouts: 4.99 us -> none
    convert_element_type x3 -> x0, other arithmetic: 3.79 us -> none  [the longest x1 1.55 us: local(): swap(expand_weight).astype(BF)]
    reduce_sum x2 -> x0, other arithmetic: 2.7 us -> none  [local(): total_square = jnp.sum(back['norm']) + jnp.sum(gains_sum * gains_sum)]
where the time goes in v2:
time: 220 us
  Pallas kernels  218 us (99%)
    pallas_call x3, Pallas kernels, call(): pl.pallas_call(kernel, out_shape=tuple((jax.ShapeDtypeStruct(*outs[n][1:]...  218 us

profile of v2, /device:TPU:1, one launch (start us, length us, event | category | flops | bytes accessed | tf_op | source)
XLA Modules:
  0.0 219.8 jit_solution(9925701083885212691)
XLA Ops:
  1.3 100.4 %shard_map.322 = (bf16[4,2,2,144,768]{4,3,2,1,0:T(8,128)(2,1)}, bf16[4,2,2,48,768]{4,3,2,1,0:T(8,128)(2,1)}, bf16[3,2,4,4,4,24,256]{6,5,4,3,2,1,0:T(8,128)(2,1)}...) custom-call(f32[2,4,6]{2,1,0:T(4,128)} %refs_17_.1, ...), custom_call_target="tpu_custom_call" | custom-call | tf_op jit(solution)/shard_map/pallas_call | solution.py:979
  101.7 114.4 %shard_map.323 = (f32[256,768]{1,0:T(8,128)}, f32[8,128]{1,0:T(8,128)}, f32[2,3,24,768]{3,2,1,0:T(8,128)}, f32[8,768]{1,0:T(8,128)}) custom-call(bf16[256,768]{1,0:T(8,128)(2,1)} %refs_0_.3, s32[1]{0:T(128)S(6)} %copy.37.refs_2_.refs_1_, bf16[192,192]{1,0:T(8,128)(2,1)} %constant.2.clone.refs_3_.refs_2_, bf16[256,768]{1,0:T(8,128)(2,1)} %refs_3_.2, ...), custom_call_target="tpu_custom_call" | custom-call | tf_op jit(solution)/shard_map/pallas_call | solution.py:979
  216.1 3.4 %shard_map.324 = (f32[256,768]{1,0:T(8,128)}, bf16[256,768]{1,0:T(8,128)(2,1)}, f32[1,1]{1,0:T(1,128)}, f32[18,2,768]{2,1,0:T(2,128)}, f32[6,2,768]{2,1,0:T(2,12...) custom-call(f32[256,768]{1,0:T(8,128)} %get-tuple-element.89.refs_0_, ...), custom_call_target="tpu_custom_call" | custom-call | tf_op jit(solution)/shard_map/pallas_call | solution.py:979

commit v3 on v2

--- a/solution.py
+++ b/solution.py
@@ -81,19 +81,6 @@
             going.append(self.step(src_of(a, b), dst_of(a, b), step))
         return going
 
-    def plane_at_once(self, axes, src_of, landing):
-        i = self.n
-        self.n += 1
-        for n, (a, b) in enumerate(CORNERS):
-            step = [0, 0, 0, 0]
-            step[axes[0]], step[axes[1]] = a, b
-            pltpu.make_async_remote_copy(src_ref=src_of(a, b), dst_ref=landing.at[n], send_sem=self.ss.at[i], recv_sem=self.rs.at[i],
-                device_id=device_at(*stepped(self.co, step)), device_id_type=MESH).start()
-        whole = pltpu.make_async_remote_copy(src_ref=landing, dst_ref=landing, send_sem=self.ss.at[i], recv_sem=self.rs.at[i],
-            device_id=device_at(*moved(self.co, 3, 1)), device_id_type=MESH)
-        self.out.append(whole)
-        return whole
-
     def sent(self, copies):
         for cp in copies:
             cp.wait_send()
@@ -102,6 +89,7 @@
     def drain(self):
         for cp in self.out:
             cp.wait_send()
+        self.out = []
 
 class Local:
     def __init__(self, sems):
@@ -338,6 +326,7 @@
 def backward_second(s, gains):
     for name in ("dstream", "ws", "raised", "we", "normed2"):
         s.need(name)
+
     s.low[...] = s.dstream[...].astype(BF)
     s.acc[...] = jnp.zeros((T, D), F32)
     def step(t):
@@ -606,10 +595,6 @@
         c = self.co[3]
         self.six = [self.link.send(self.dst.at[t, c], self.dst.at[t, c], 3, 1) for t in range(3)]
 
-    def sent(self):
-        groups = (*self.one, *self.two, self.three, *self.four, self.five, self.six)
-        self.link.sent([cp for g in groups for cp in g])
-
     def ready(self):
         for cp in self.six:
             cp.wait_recv()
@@ -619,7 +604,7 @@
     x, y, z, c = co
     length = ins.length[0]
     fetch(ins, s, loc, ("stream",))
-    targets = [[s.slots.at[0], s.we, s.ws], [s.slots.at[1], out.top_we, out.top_ws]]
+    targets = [[s.slots.at[0], s.we, s.ws], [s.slots.at[1], s.later_we, s.later_ws]]
     items = []
     for l in range(2):
         rows = jnp.concatenate([ins.joint[:, l, :], ins.output[:, l, :]], axis=0)
@@ -656,12 +641,14 @@
         for n in names:
             done.append(loc.copy(getattr(s, n), getattr(out, prefix + n)))
 
-    for name in ("slab", "slab_on"):
-        for item in items:
-            getattr(item, name)()
-        if name == "slab":
-            gain_sum.second()
+    for item in items:
+        item.slab()
+    gain_sum.second()
+    for item in items[:3]:
+        item.slab_on()
     items[0].block()
+    for item in items[3:]:
+        item.slab_on()
     items[1].block()
     out.gains_all[...] = gain_sum.total()
     gains = out.gains_all[0:4]
@@ -674,13 +661,13 @@
     s.need("stream")
     first = forward_first(s, gains, length)
     next(first)
+    step(3)
     next(first)
-    step(3)
     run(first)
+    step(4)
     items[1].ready()
     second = forward_second(s, gains)
     next(second)
-    step(4)
     items[2].ready()
     save("normed", "proj", "probs", "attended", "mid", "normed2", "raised")
     run(second)
@@ -690,30 +677,27 @@
     done.clear()
     save("we", "ws")
     done.append(loc.copy(s.second, out.top_stream))
-    top = Names(**{k: v for k, v in s.__dict__.items() if k not in ("coming", "sums", "stream", "met")}, stream=s.second)
+    top = Names(**{k: v for k, v in s.__dict__.items() if k not in ("coming", "sums", "stream", "met", "we", "ws")}, stream=s.second, we=s.later_we,
+        ws=s.later_ws)
     gains = out.gains_all[4:8]
+    step(5)
     items[3].ready()
     compact(s.slots.at[1], s.wj, s.wo, perm[...])
     save("wj", "wo", prefix="top_")
-    step(5)
     first = forward_first(top, gains, length)
     next(first)
     step(6)
     items[4].ready()
-    items[1].sent()
-    for cp in done:
-        cp.wait()
-    done.clear()
-    top.coming["we"] = [loc.copy(out.top_we, s.we)]
+    done.append(loc.copy(s.later_we, out.top_we))
     next(first)
     run(first)
     save("normed", "proj", "probs", "attended", "mid", prefix="top_")
     second = forward_second(top, gains)
     next(second)
     save("normed2", "raised", prefix="top_")
+    link.drain()
     items[5].ready()
-    items[2].sent()
-    top.coming["ws"] = [loc.copy(out.top_ws, s.ws)]
+    done.append(loc.copy(s.later_ws, out.top_ws))
     run(second)
     out.layer_output[...] = s.next[...].astype(BF)
     for cp in done:
@@ -770,23 +754,38 @@
         self.link, self.s, self.l, self.first, self.count = link, s, l, first, count
         self.which = pl.ds(first, count)
 
+    def row(self, t, q):
+        block = self.s.r2.at[self.l, t, 0]
+        return block.at[:, q, self.which] if RINGS[t][1] == PLANES[t][1] else block.at[q, :, self.which]
+
     def send(self):
         co, self.going = self.link.co, []
         for t in range(3):
-            u, v = PLANES[t]
-            block = self.s.r2.at[self.l, t, 0]
-            pick = lambda a, b: block.at[lax.rem(co[u] + a, 4), lax.rem(co[v] + b, 4), self.which]
-            self.going.append(self.link.plane_at_once(PLANES[t], pick, self.s.u1.at[self.l, t, :, self.which]))
+            v = RINGS[t][1]
+            self.going.append([self.link.send(self.row(t, moved(co, v, k)[v]), self.s.m1.at[self.l, t, k - 1, :, self.which], v, k)
+                for k in (2, 1, 3)])
+
+    def cross(self):
+        co, self.last = self.link.co, []
+        for t in range(3):
+            for cp in self.going[t]:
+                cp.wait_recv()
+            u, v = RINGS[t]
+            got = [self.s.m1.at[self.l, t, k, :, self.which] for k in range(3)]
+            acc(got[0], [self.row(t, co[v])] + got, (4, self.count))
+            self.last.append([self.link.send(self.s.m1.at[self.l, t, 0, moved(co, u, k)[u], self.which],
+                self.s.u2.at[self.l, t, k - 1, self.which], u, k) for k in (2, 1, 3)])
 
     def final(self, square):
         co = self.link.co
         for t in range(3):
-            u, v = PLANES[t]
-            self.going[t].wait_recv()
+            for cp in self.last[t]:
+                cp.wait_recv()
+            u = RINGS[t][0]
             for w in range(self.first, self.first + self.count):
-                g = self.s.r2[self.l, t, 0, co[u], co[v], w].astype(F32)
-                for k in range(15):
-                    g = g + self.s.u1[self.l, t, k, w].astype(F32)
+                g = self.s.m1[self.l, t, 0, co[u], w].astype(F32)
+                for k in range(3):
+                    g = g + self.s.u2[self.l, t, k, w].astype(F32)
                 self.s.grads[self.l, w, :, third(t)] = g
                 g = g * g
                 g = g[0:8] + g[8:16] + g[16:24]
@@ -819,89 +818,89 @@
     run(backward_second(top, g))
     s.met()
     pairs[1].send("ws")
+    pairs[1].send("we")
     bring(base, "", "raised", "normed2", "mid")
     for k, _ in enumerate(backward_first(top, g, length)):
         if k == 0:
-            pairs[1].send("we")
             pairs[1].send("wo")
-        if k == 1:
+        if k == 3:
+            bring(base, "", "attended", "proj", "probs")
             pairs[1].join("ws")
             up[2].far()
             up[2].near()
-        if k == 2:
-            pairs[1].join("we")
-            up[1].far()
-            up[1].near()
-        if k == 3:
-            bring(base, "", "attended", "proj", "probs")
         if k == 4:
             pairs[1].send("wj", pl.ds(0, 2))
-            up[2].onward()
         if k == 5:
             pairs[1].send("wj", pl.ds(2, 2))
-    up[1].onward()
     bring(base, "", "normed")
+    pairs[1].join("we")
+    up[1].far()
+    up[1].near()
     square = None
     base.coming["dstream"] = []
     g = ins.gains[0:4]
     for k, _ in enumerate(backward_second(base, g)):
         if k == 0:
+            up[2].onward()
+        if k == 1:
             pairs[1].join_rows(perm[...])
             up[0].far()
             up[0].near()
             link.sent(pairs[1].copies["wj"] + pairs[1].copies["wo"])
             bring(base, "", "wj", "wo")
             pl.semaphore_signal(s.credit, inc=1, device_id=device_at(*moved(co, 3, 1)), device_id_type=MESH)
-            up[2].collect()
+            up[1].onward()
+    pl.semaphore_wait(s.credit, 1)
+    pairs[0].send("ws")
+    pairs[0].send("we")
+    up[2].collect()
+    for k, _ in enumerate(backward_first(base, g, length)):
+        if k == 0:
+            pairs[0].send("wo")
+            up[0].onward()
         if k == 1:
             up[1].collect()
-        if k == 2:
-            up[0].onward()
-    pl.semaphore_wait(s.credit, 1)
-    pairs[0].send("ws")
-    for k, _ in enumerate(backward_first(base, g, length)):
-        if k == 0:
-            pairs[0].send("we")
-            pairs[0].send("wo")
-            up[0].collect()
-            top_end.send()
-        if k == 1:
+        if k == 3:
             pairs[0].join("ws")
             low[2].far()
             low[2].near()
-        if k == 2:
+            up[0].collect()
+            top_end.send()
+        if k == 4:
+            pairs[0].send("wj", pl.ds(0, 2))
+        if k == 5:
+            pairs[0].send("wj", pl.ds(2, 2))
             pairs[0].join("we")
             low[1].far()
             low[1].near()
-        if k == 3:
-            square = top_end.final(square)
-            up[0].sent()
-        if k == 4:
-            pairs[0].send("wj", pl.ds(0, 2))
-            low[2].onward()
-        if k == 5:
-            pairs[0].send("wj", pl.ds(2, 2))
-            low[1].onward()
+            top_end.cross()
     gain_sum = WideSum(link, s.gwide, s.gdeep)
     gain_sum.first(jnp.concatenate([gains_of(base.sums), gains_of(top.sums)], axis=0))
     copies = [loc.copy(s.dstream, out.dstream)]
-    low[2].collect()
+    low[2].onward()
+    up[0].sent()
     pairs[0].join_rows(perm[...])
     low[0].far()
     low[0].near()
+    low[1].onward()
+    low[2].collect()
+    gain_sum.second()
+    low[0].onward()
     low[1].collect()
     ff_end.send()
-    low[0].onward()
-    gain_sum.second()
-    square = ff_end.final(square)
+    square = top_end.final(square)
     low[0].collect()
     row_end.send()
+    ff_end.cross()
     gains_sum = gain_sum.total()
     out.gains_sum[...] = gains_sum
+    row_end.cross()
+    square = ff_end.final(square)
     square = row_end.final(square)
     copies.append(loc.copy(s.grads, out.grads))
     norm_sum = WideSum(link, s.nwide, s.ndeep)
     norm_sum.first(square)
+    link.drain()
     norm_sum.second()
     whole = norm_sum.total()
     norm = jnp.sqrt(jnp.sum(jnp.sum(whole, axis=0, keepdims=True), axis=1, keepdims=True)
@@ -1011,7 +1010,8 @@
     row = ((T, D), F32)
     outs = {**hbm(WEIGHTS), **hbm(SAVED), **hbm(WEIGHTS, "top_"), **hbm(SAVED, "top_"), "top_stream": (ANY, *row),
         "gains_all": (VMEM, (8, D), F32), "layer_output": (VMEM, (T, D), BF)}
-    own = dict(stream=((T, D), BF), second=row, piece=((2, 3, 24, D), BF), slots=((2, 3, 2, 4, 4, 4, 24, 256), BF))
+    own = dict(stream=((T, D), BF), second=row, piece=((2, 3, 24, D), BF), slots=((2, 3, 2, 4, 4, 4, 24, 256), BF), later_we=WEIGHTS["we"],
+        later_ws=WEIGHTS["ws"])
     return call(first_body, ins, outs, {**WEIGHTS, **SAVED, **ONCE, **own, **SUMS}, 64, 272, 0, ((0, 1),))
 
 
@@ -1023,10 +1023,10 @@
     outs = dict(dstream=(ANY, (T, D), F32), norm=(VMEM, (8, 128), F32), grads=(ANY, (2, 3, 24, D), F32),
         gains_sum=(VMEM, (8, D), F32))
     own = dict(stream=((T, D), BF), top_stream=((T, D), F32), ga=OWN, r1=((2, 3, 3, 2, 2, 4, 24, 256), BF),
-        r2=((2, 3, 2, 4, 4, 3, 24, 256), BF), u1=((2, 3, 15, 3, 24, 256), BF), grads=((2, 3, 24, D), F32),
+        r2=((2, 3, 2, 4, 4, 3, 24, 256), BF), m1=((2, 3, 3, 4, 3, 24, 256), BF), u2=((2, 3, 3, 3, 24, 256), BF), grads=((2, 3, 24, D), F32),
         nwide=((4, 4, 8, 128), F32), ndeep=((4, 2, 8, 128), F32))
     weights = {"top_" + k: WEIGHTS[k] for k in ("we", "ws")}
-    return call(second_body, ins, outs, {**WEIGHTS, **weights, **SAVED, **BACK, **own, **SUMS, **SIBLING}, 64, 200, 1, PLANES,
+    return call(second_body, ins, outs, {**WEIGHTS, **weights, **SAVED, **BACK, **own, **SUMS, **SIBLING}, 64, 240, 1, ((0, 1),),
         credit=True)
 
 

time: 220 us -> 209 us (0.950)
  Pallas kernels: 218 us -> 207 us
    pallas_call x3, Pallas kernels: 218 us -> 207 us  [call(): pl.pallas_call(kernel, out_shape=tuple((jax.ShapeDtypeStruct(*outs[n][1:]...]
where the time goes in v3:
time: 209 us
  Pallas kernels  207 us (99%)
    pallas_call x3, Pallas kernels, call(): pl.pallas_call(kernel, out_shape=tuple((jax.ShapeDtypeStruct(*outs[n][1:]...  207 us

profile of v3, /device:TPU:1, one launch (start us, length us, event | category | flops | bytes accessed | tf_op | source)
XLA Modules:
  0.0 208.5 jit_solution(12060851688934618052)
XLA Ops:
  1.3 101.7 %shard_map.322 = (bf16[4,2,2,144,768]{4,3,2,1,0:T(8,128)(2,1)}, bf16[4,2,2,48,768]{4,3,2,1,0:T(8,128)(2,1)}, bf16[3,2,4,4,4,24,256]{6,5,4,3,2,1,0:T(8,128)(2,1)}...) custom-call(f32[2,4,6]{2,1,0:T(4,128)} %refs_17_.1, ...), custom_call_target="tpu_custom_call" | custom-call | tf_op jit(solution)/shard_map/pallas_call | solution.py:978
  103.0 102.0 %shard_map.323 = (f32[256,768]{1,0:T(8,128)}, f32[8,128]{1,0:T(8,128)}, f32[2,3,24,768]{3,2,1,0:T(8,128)}, f32[8,768]{1,0:T(8,128)}) custom-call(bf16[256,768]{1,0:T(8,128)(2,1)} %refs_0_.3, s32[1]{0:T(128)S(6)} %copy.37.refs_2_.refs_1_, bf16[192,192]{1,0:T(8,128)(2,1)} %constant.2.clone.refs_3_.refs_2_, bf16[256,768]{1,0:T(8,128)(2,1)} %refs_3_.2, ...), custom_call_target="tpu_custom_call" | custom-call | tf_op jit(solution)/shard_map/pallas_call | solution.py:978
  204.9 3.4 %shard_map.324 = (f32[256,768]{1,0:T(8,128)}, bf16[256,768]{1,0:T(8,128)(2,1)}, f32[1,1]{1,0:T(1,128)}, f32[18,2,768]{2,1,0:T(2,128)}, f32[6,2,768]{2,1,0:T(2,12...) custom-call(f32[256,768]{1,0:T(8,128)} %get-tuple-element.89.refs_0_, ...), custom_call_target="tpu_custom_call" | custom-call | tf_op jit(solution)/shard_map/pallas_call | solution.py:978

commit v4 on v3

--- a/solution.py
+++ b/solution.py
@@ -330,6 +330,7 @@
     s.low[...] = s.dstream[...].astype(BF)
     s.acc[...] = jnp.zeros((T, D), F32)
     def step(t):
+        t = lax.rem(t + s.flip, 8)
         at = tile(t, FT)
         dh = dot_nt(s.low[:, third(0)], slots_at(s.ws, 0, t))
         for n in (1, 2):
@@ -345,6 +346,9 @@
         put_slots(s.we, t, dot_tn(dr, s.normed2[...]))
     pieces = 4 * D // FT // 2
     for piece in range(pieces):
+        if piece == pieces // 2:
+            for name in ("ws_later", "raised_later", "we_later"):
+                s.need(name)
         loop(2, lambda t: step(t + 2 * piece))
         if piece < pieces - 1:
             yield
@@ -801,6 +805,7 @@
     base = Names(**shared)
     top = Names(**{**shared, **{k: getattr(s, "top_" + k) for k in ("we", "ws", "stream")}})
     layers = (base, top)
+    base.flip = top.flip = 4 * (1 - c)
     pairs = [Pair(n, link, c) for n in layers]
     sums = [[Reduce(link, s, l, w, (n.ga, n.we.at[:, c], n.ws.at[:, c])[w]) for w in range(3)] for l, n in enumerate(layers)]
     low, up = sums
@@ -811,31 +816,42 @@
         for name in names:
             n.coming[name] = [loc.copy(getattr(ins, prefix + name), getattr(n, name))]
 
-    bring(top, "top_", "ws", "raised", "we", "normed2", "mid", "wo", "attended", "proj", "probs", "wj", "normed", "stream")
+    def bring_half(n, prefix, h, *names):
+        for name in names:
+            half = 1 - c if h == 0 else c
+            at = (slice(None), tile(half, 2 * D) if name == "raised" else half)
+            n.coming[name + "_later" * h] = [loc.copy(getattr(ins, prefix + name).at[at], getattr(n, name).at[at])]
+
+    bring_half(top, "top_", 0, "ws", "raised", "we")
+    bring(top, "top_", "normed2")
+    bring_half(top, "top_", 1, "ws", "raised", "we")
+    bring(top, "top_", "mid", "wo", "attended", "proj", "probs", "wj", "normed", "stream")
     bring(base, "", "we", "ws", "stream")
     s.dstream[...] = jnp.where(live_rows(length), ins.cotangent[...].astype(F32), 0.0)
     g = ins.gains[4:8]
-    run(backward_second(top, g))
-    s.met()
-    pairs[1].send("ws")
-    pairs[1].send("we")
+    for k, _ in enumerate(backward_second(top, g)):
+        if k == 1:
+            s.met()
+            pairs[1].send("ws")
+            pairs[1].send("we")
     bring(base, "", "raised", "normed2", "mid")
     for k, _ in enumerate(backward_first(top, g, length)):
         if k == 0:
             pairs[1].send("wo")
-        if k == 3:
-            bring(base, "", "attended", "proj", "probs")
+        if k == 1:
             pairs[1].join("ws")
             up[2].far()
             up[2].near()
+        if k == 3:
+            bring(base, "", "attended", "proj", "probs")
+            pairs[1].join("we")
+            up[1].far()
+            up[1].near()
         if k == 4:
             pairs[1].send("wj", pl.ds(0, 2))
         if k == 5:
             pairs[1].send("wj", pl.ds(2, 2))
     bring(base, "", "normed")
-    pairs[1].join("we")
-    up[1].far()
-    up[1].near()
     square = None
     base.coming["dstream"] = []
     g = ins.gains[0:4]
@@ -850,9 +866,10 @@
             bring(base, "", "wj", "wo")
             pl.semaphore_signal(s.credit, inc=1, device_id=device_at(*moved(co, 3, 1)), device_id_type=MESH)
             up[1].onward()
-    pl.semaphore_wait(s.credit, 1)
-    pairs[0].send("ws")
-    pairs[0].send("we")
+        if k == 2:
+            pl.semaphore_wait(s.credit, 1)
+            pairs[0].send("ws")
+            pairs[0].send("we")
     up[2].collect()
     for k, _ in enumerate(backward_first(base, g, length)):
         if k == 0:
@@ -860,29 +877,29 @@
             up[0].onward()
         if k == 1:
             up[1].collect()
-        if k == 3:
             pairs[0].join("ws")
             low[2].far()
             low[2].near()
+        if k == 3:
             up[0].collect()
             top_end.send()
+            pairs[0].join("we")
+            low[1].far()
+            low[1].near()
         if k == 4:
             pairs[0].send("wj", pl.ds(0, 2))
         if k == 5:
             pairs[0].send("wj", pl.ds(2, 2))
-            pairs[0].join("we")
-            low[1].far()
-            low[1].near()
-            top_end.cross()
+            low[2].onward()
     gain_sum = WideSum(link, s.gwide, s.gdeep)
     gain_sum.first(jnp.concatenate([gains_of(base.sums), gains_of(top.sums)], axis=0))
     copies = [loc.copy(s.dstream, out.dstream)]
-    low[2].onward()
     up[0].sent()
     pairs[0].join_rows(perm[...])
     low[0].far()
     low[0].near()
     low[1].onward()
+    top_end.cross()
     low[2].collect()
     gain_sum.second()
     low[0].onward()

time: 209 us -> 205 us (0.981)
  Pallas kernels: 207 us -> 203 us
    pallas_call x3, Pallas kernels: 207 us -> 203 us  [call(): pl.pallas_call(kernel, out_shape=tuple((jax.ShapeDtypeStruct(*outs[n][1:]...]
where the time goes in v4:
time: 205 us; the launch traced here: 204 us
  Pallas kernels  203 us (99%)
    pallas_call x3, Pallas kernels, call(): pl.pallas_call(kernel, out_shape=tuple((jax.ShapeDtypeStruct(*outs[n][1:]...  203 us

profile of v4, /device:TPU:1, one launch (start us, length us, event | category | flops | bytes accessed | tf_op | source)
XLA Modules:
  0.0 204.4 jit_solution(15538706365156949918)
XLA Ops:
  1.3 101.7 %shard_map.322 = (bf16[4,2,2,144,768]{4,3,2,1,0:T(8,128)(2,1)}, bf16[4,2,2,48,768]{4,3,2,1,0:T(8,128)(2,1)}, bf16[3,2,4,4,4,24,256]{6,5,4,3,2,1,0:T(8,128)(2,1)}...) custom-call(f32[2,4,6]{2,1,0:T(4,128)} %refs_17_.1, ...), custom_call_target="tpu_custom_call" | custom-call | tf_op jit(solution)/shard_map/pallas_call | solution.py:995
  103.0 97.8 %shard_map.323 = (f32[256,768]{1,0:T(8,128)}, f32[8,128]{1,0:T(8,128)}, f32[2,3,24,768]{3,2,1,0:T(8,128)}, f32[8,768]{1,0:T(8,128)}) custom-call(bf16[256,768]{1,0:T(8,128)(2,1)} %refs_0_.3, s32[1]{0:T(128)S(6)} %copy.37.refs_2_.refs_1_, bf16[192,192]{1,0:T(8,128)(2,1)} %constant.2.clone.refs_3_.refs_2_, bf16[256,768]{1,0:T(8,128)(2,1)} %refs_3_.2, ...), custom_call_target="tpu_custom_call" | custom-call | tf_op jit(solution)/shard_map/pallas_call | solution.py:995
  200.7 3.4 %shard_map.324 = (f32[256,768]{1,0:T(8,128)}, bf16[256,768]{1,0:T(8,128)(2,1)}, f32[1,1]{1,0:T(1,128)}, f32[18,2,768]{2,1,0:T(2,128)}, f32[6,2,768]{2,1,0:T(2,12...) custom-call(f32[256,768]{1,0:T(8,128)} %get-tuple-element.89.refs_0_, ...), custom_call_target="tpu_custom_call" | custom-call | tf_op jit(solution)/shard_map/pallas_call | solution.py:995

commit v5 on v4

--- a/solution.py
+++ b/solution.py
@@ -291,7 +291,10 @@
     wj = s.wj.reshape(3 * D, D)
     def project(t):
         s.proj[:, tile(t, 256)] = dot_nt(s.normed[...], wj[tile(t, 256), :]).astype(BF)
-    loop(9, project)
+    def three(n):
+        for k in range(3):
+            project(3 * n + k)
+    loop(3, three)
     yield
     attention(s.proj, s.probs, s.attended, s.bias, length)
     yield
@@ -530,7 +533,11 @@
             rows = dot_nn(perm, slots[t, c, x, pl.ds(2 * h, 2)].reshape(192, 256)).astype(BF)
             wj[x, h, c, :, third(t)] = rows[:144]
             wo[x, h, c, :, third(t)] = rows[144:]
-    loop(16, step)
+
+    def four(n):
+        for k in range(4):
+            step(4 * n + k)
+    loop(4, four)
 
 
 class Gather:

time: 205 us -> 202 us (0.985)
  Pallas kernels: 203 us -> 200 us
    pallas_call x3, Pallas kernels: 203 us -> 200 us  [call(): pl.pallas_call(kernel, out_shape=tuple((jax.ShapeDtypeStruct(*outs[n][1:]...]
where the time goes in v5:
time: 202 us
  Pallas kernels  200 us (99%)
    pallas_call x3, Pallas kernels, call(): pl.pallas_call(kernel, out_shape=tuple((jax.ShapeDtypeStruct(*outs[n][1:]...  200 us

profile of v5, /device:TPU:1, one launch (start us, length us, event | category | flops | bytes accessed | tf_op | source)
XLA Modules:
  0.0 201.6 jit_solution(3805816646313325441)
XLA Ops:
  1.3 96.0 %shard_map.322 = (bf16[4,2,2,144,768]{4,3,2,1,0:T(8,128)(2,1)}, bf16[4,2,2,48,768]{4,3,2,1,0:T(8,128)(2,1)}, bf16[3,2,4,4,4,24,256]{6,5,4,3,2,1,0:T(8,128)(2,1)}...) custom-call(f32[2,4,6]{2,1,0:T(4,128)} %refs_17_.1, ...), custom_call_target="tpu_custom_call" | custom-call | tf_op jit(solution)/shard_map/pallas_call | solution.py:1002
  97.3 100.7 %shard_map.323 = (f32[256,768]{1,0:T(8,128)}, f32[8,128]{1,0:T(8,128)}, f32[2,3,24,768]{3,2,1,0:T(8,128)}, f32[8,768]{1,0:T(8,128)}) custom-call(bf16[256,768]{1,0:T(8,128)(2,1)} %refs_0_.3, s32[1]{0:T(128)S(6)} %copy.37.refs_2_.refs_1_, bf16[192,192]{1,0:T(8,128)(2,1)} %constant.2.clone.refs_3_.refs_2_, bf16[256,768]{1,0:T(8,128)(2,1)} %refs_3_.2, ...), custom_call_target="tpu_custom_call" | custom-call | tf_op jit(solution)/shard_map/pallas_call | solution.py:1002
  198.0 3.4 %shard_map.324 = (f32[256,768]{1,0:T(8,128)}, bf16[256,768]{1,0:T(8,128)(2,1)}, f32[1,1]{1,0:T(1,128)}, f32[18,2,768]{2,1,0:T(2,128)}, f32[6,2,768]{2,1,0:T(2,12...) custom-call(f32[256,768]{1,0:T(8,128)} %get-tuple-element.89.refs_0_, ...), custom_call_target="tpu_custom_call" | custom-call | tf_op jit(solution)/shard_map/pallas_call | solution.py:1002
